TPU v7x, 512 devices: a whole 4x4x16 slice. The times are simulated.
512 devices in a mesh: ctx: 64 (over z, x), head: 8 (over y, core).
Axes of the slice: x: 4, y: 4, z: 16, core: 2. Of those that a mesh axis runs over, the one named last changes fastest.
Arguments:
- queries: bfloat16 [32768, 8192], P(('ctx', 'head')), may hold values from -170 to 170
- keys: bfloat16 [32768, 1024], P(('ctx', 'head')), may hold values from -6 to 6
- values: bfloat16 [32768, 1024], P(('ctx', 'head')), may hold values from -6 to 6
- doc_ids: int32 [32768], replicated, may hold values from 0 to 31, never falling along the last dimension, each value on 1 to 2561 neighbouring positions
Outputs:
- attended: bfloat16 [32768, 8192], P(('ctx', 'head'))
Inputs may be any that keep to these rules, and one draw needn't show every extreme that they name: `doc_ids`: documents are contiguous runs, each of 1 to 2561 tokens, one exactly 2561.
All inputs are finite; a program needn't handle non-finite values.
Results may differ from a plain program's by a relative error of at most 0.0037.
Values may be sent and summed in bfloat16 or wider, within the bound.
No kernel may reach another device: no remote copies, remote signals or barrier semaphores. Data moves between devices by JAX's collectives and lax.ppermute only.
A program may use at most 64 MiB of HBM per device.

v0:
```python
import math

import jax
import jax.numpy as jnp
from jax import lax
from jax.sharding import PartitionSpec as P

HD = 128
REACH = 5


def passed_along(value, axis, steps):
    count = lax.axis_size(axis)
    initial, last = (max(0, -steps), min(count, count - steps))
    return lax.ppermute(value, axis, [(source, source + steps) for source in range(initial, last)])


def attend(query_rows, key_rows, value_rows, visible):
    row_count = query_rows.shape[0]
    query_heads = query_rows.shape[1] // HD
    scaling = 1.0 / math.sqrt(HD)

    def one_head(head_number):
        query_head = lax.dynamic_slice_in_dim(query_rows, head_number * HD, HD, 1)
        scores = (
            lax.dot_general(
                query_head, key_rows, (((1,), (1,)), ((), ())), preferred_element_type=jnp.float32
            )
            * scaling
        )
        scores = jnp.where(visible, scores, -jnp.inf)
        peak = jnp.max(scores, axis=1, keepdims=True)
        weights = jnp.exp(scores - peak)
        totals = jnp.sum(weights, axis=1, keepdims=True)
        mixed = jnp.dot(
            weights.astype(jnp.bfloat16), value_rows, preferred_element_type=jnp.float32
        )
        return (mixed / totals).astype(jnp.bfloat16)

    stacked = lax.map(one_head, jnp.arange(query_heads, dtype=jnp.int32))
    return jnp.transpose(stacked, (1, 0, 2)).reshape(row_count, query_heads * HD)


def widen(key_rows, value_rows):
    pieces = [(key_rows, value_rows)]
    for distance in range(1, REACH + 1):
        pieces.append(passed_along((key_rows, value_rows), "ctx", distance))
    ordered = pieces[::-1]
    key_window = jnp.concatenate([piece[0] for piece in ordered], axis=0)
    value_window = jnp.concatenate([piece[1] for piece in ordered], axis=0)
    return (key_window, value_window)


def body(queries, keys, values, doc_ids):
    tok_count = queries.shape[0]
    block_rows = tok_count * lax.axis_size("head")
    window_len = (REACH + 1) * block_rows
    ctx_number = lax.axis_index("ctx")
    block_first = ctx_number * block_rows
    doc_pad = jnp.concatenate([jnp.full((REACH * block_rows,), -1, jnp.int32), doc_ids])
    key_docs = lax.dynamic_slice_in_dim(doc_pad, block_first, window_len, 0)
    key_pos = block_first - REACH * block_rows + jnp.arange(window_len, dtype=jnp.int32)
    query_local, key_local, value_local = (
        lax.all_to_all(queries, "head", split_axis=1, concat_axis=0, tiled=True),
        lax.all_to_all(keys, "head", split_axis=1, concat_axis=0, tiled=True),
        lax.all_to_all(values, "head", split_axis=1, concat_axis=0, tiled=True),
    )
    key_window, value_window = widen(key_local, value_local)
    query_pos = block_first + jnp.arange(block_rows, dtype=jnp.int32)
    query_docs = lax.dynamic_slice_in_dim(doc_ids, block_first, block_rows, 0)
    visible = (
        (query_docs[:, None] == key_docs[None, :])
        & (key_pos[None, :] <= query_pos[:, None])
        & (key_pos[None, :] >= 0)
    )
    local_out = attend(query_local, key_window, value_window, visible)
    return lax.all_to_all(local_out, "head", split_axis=0, concat_axis=1, tiled=True)


def solution(mesh):
    return jax.shard_map(
        body,
        mesh=mesh,
        in_specs=(
            P(("ctx", "head"), None),
            P(("ctx", "head"), None),
            P(("ctx", "head"), None),
            P(),
        ),
        out_specs=P(("ctx", "head"), None),
        check_vma=False,
    )
```

profile of v0, /device:TPU:32, one launch (start us, length us, event | category | flops | bytes accessed | tf_op | source)
XLA Modules:
  0.0 148.9 jit_solution(17708207708938978232)
XLA Ops:
  1.6 4.5 %all-to-all-start.1 = ((bf16[64,8,128]{2,0,1:T(8,128)(2,1)}), bf16[64,8,128]{2,0,1:T(8,128)(2,1)S(1)}, u32[]{:S(2)}, u32[]{:S(2)}) async-start(bf16[64,8,128]{2,0,1:T(8,128)(2,1)} %copy_bitcast_fusion.2), calls=%async_computation.1 | async-start | bytes 262144 | tf_op jit(solution)/shard_map/all_to_all | solution.py:65
  6.1 1.6 %copy_bitcast_fusion.1 = bf16[64,8,128]{2,0,1:T(8,128)(2,1)} fusion(bf16[64,1024]{1,0:T(8,128)(2,1)} %param.8), kind=kLoop, calls=%fused_computation.15 | loop fusion | bytes 262144 | tf_op jit(solution)/shard_map/all_to_all | solution.py:66
  8.4 3.8 %all-to-all-done.1 = bf16[64,8,128]{2,0,1:T(8,128)(2,1)S(1)} async-done(((bf16[64,8,128]{2,0,1:T(8,128)(2,1)}), bf16[64,8,128]{2,0,1:T(8,128)(2,1)S(1)}, u32[]{:S(2)}, u32[]{:S(2)}) %all-to-all-start.1) | async-done | bytes 131104 | tf_op jit(solution)/shard_map/all_to_all | solution.py:65
  12.2 3.4 %all-to-all-start.2 = ((bf16[64,8,128]{2,0,1:T(8,128)(2,1)}), bf16[64,8,128]{2,0,1:T(8,128)(2,1)S(1)}, u32[]{:S(2)}, u32[]{:S(2)}) async-start(bf16[64,8,128]{2,0,1:T(8,128)(2,1)} %copy_bitcast_fusion.1), calls=%async_computation.2 | async-start | bytes 262144 | tf_op jit(solution)/shard_map/all_to_all | solution.py:66
  15.6 4.8 %collective-permute-start = (bf16[512,128]{1,0:T(8,128)(2,1)S(1)}, bf16[512,128]{1,0:T(8,128)(2,1)S(1)}, u32[]{:S(2)}, u32[]{:S(2)}) collective-permute-start(bf16[512,128]{1,0:T(8,128)(2,1)S(1)} %bitcast.46), channel_id=1, source_target_pairs={{0,40},{8,48},{16,56},{24,64},{32,72},{40,80},{48,88},{56,96},{64,... | collective-permute-start | bytes 393224 | tf_op jit(solution)/shard_map/ppermute | solution.py:15
  20.4 3.8 %collective-permute-start.1 = (bf16[512,128]{1,0:T(8,128)(2,1)S(1)}, bf16[512,128]{1,0:T(8,128)(2,1)S(1)}, u32[]{:S(2)}, u32[]{:S(2)}) collective-permute-start(bf16[512,128]{1,0:T(8,128)(2,1)S(1)} %bitcast.47), channel_id=1, source_target_pairs={{0,32},{8,40},{16,48},{24,56},{32,64},{40,72},{48,80},{56,88},{64,... | collective-permute-start | bytes 393224 | tf_op jit(solution)/shard_map/ppermute | solution.py:15
  25.0 2.3 %copy.24 = bf16[8,8,8,1024]{3,2,0,1:T(8,128)(2,1)} copy(bf16[8,8,8,1024]{3,2,1,0:T(8,128)(2,1)} %bitcast.43) | data formatting | bytes 2097152 | tf_op jit(solution)/shard_map/all_to_all | solution.py:64
  27.3 6.2 %collective-permute-start.2 = (bf16[512,128]{1,0:T(8,128)(2,1)S(1)}, bf16[512,128]{1,0:T(8,128)(2,1)S(1)}, u32[]{:S(2)}, u32[]{:S(2)}) collective-permute-start(bf16[512,128]{1,0:T(8,128)(2,1)S(1)} %bitcast.48), channel_id=1, source_target_pairs={{0,24},{8,32},{16,40},{24,48},{32,56},{40,64},{48,72},{56,80},{64,... | collective-permute-start | bytes 393224 | tf_op jit(solution)/shard_map/ppermute | solution.py:15
  33.5 3.7 %collective-permute-start.3 = (bf16[512,128]{1,0:T(8,128)(2,1)S(1)}, bf16[512,128]{1,0:T(8,128)(2,1)S(1)}, u32[]{:S(2)}, u32[]{:S(2)}) collective-permute-start(bf16[512,128]{1,0:T(8,128)(2,1)S(1)} %bitcast.49), channel_id=1, source_target_pairs={{0,16},{8,24},{16,32},{24,40},{32,48},{40,56},{48,64},{56,72},{64,... | collective-permute-start | bytes 393224 | tf_op jit(solution)/shard_map/ppermute | solution.py:15
  37.2 2.5 %collective-permute-start.4 = (bf16[512,128]{1,0:T(8,128)(2,1)S(1)}, bf16[512,128]{1,0:T(8,128)(2,1)S(1)}, u32[]{:S(2)}, u32[]{:S(2)}) collective-permute-start(bf16[512,128]{1,0:T(8,128)(2,1)S(1)} %bitcast.50), channel_id=1, source_target_pairs={{0,8},{8,16},{16,24},{24,32},{32,40},{40,48},{48,56},{56,64},{64,7... | collective-permute-start | bytes 393224 | tf_op jit(solution)/shard_map/ppermute | solution.py:15
  39.7 4.7 %all-to-all-start = ((bf16[64,8,1024]{2,0,1:T(8,128)(2,1)}), bf16[64,8,1024]{2,0,1:T(8,128)(2,1)S(1)}, u32[]{:S(2)}, u32[]{:S(2)}) async-start(bf16[64,8,1024]{2,0,1:T(8,128)(2,1)} %bitcast.33), calls=%async_computation | async-start | bytes 2097152 | tf_op jit(solution)/shard_map/all_to_all | solution.py:64
  44.4 5.7 %collective-permute-start.5 = (bf16[512,128]{1,0:T(8,128)(2,1)S(1)}, bf16[512,128]{1,0:T(8,128)(2,1)S(1)}, u32[]{:S(2)}, u32[]{:S(2)}) collective-permute-start(bf16[512,128]{1,0:T(8,128)(2,1)S(1)} %bitcast.52), channel_id=1, source_target_pairs={{0,40},{8,48},{16,56},{24,64},{32,72},{40,80},{48,88},{56,96},{64,... | collective-permute-start | bytes 393224 | tf_op jit(solution)/shard_map/ppermute | solution.py:15
  50.2 3.8 %collective-permute-start.6 = (bf16[512,128]{1,0:T(8,128)(2,1)S(1)}, bf16[512,128]{1,0:T(8,128)(2,1)S(1)}, u32[]{:S(2)}, u32[]{:S(2)}) collective-permute-start(bf16[512,128]{1,0:T(8,128)(2,1)S(1)} %bitcast.53), channel_id=1, source_target_pairs={{0,32},{8,40},{16,48},{24,56},{32,64},{40,72},{48,80},{56,88},{64,... | collective-permute-start | bytes 393224 | tf_op jit(solution)/shard_map/ppermute | solution.py:15
  54.1 4.1 %collective-permute-start.7 = (bf16[512,128]{1,0:T(8,128)(2,1)S(1)}, bf16[512,128]{1,0:T(8,128)(2,1)S(1)}, u32[]{:S(2)}, u32[]{:S(2)}) collective-permute-start(bf16[512,128]{1,0:T(8,128)(2,1)S(1)} %bitcast.54), channel_id=1, source_target_pairs={{0,24},{8,32},{16,40},{24,48},{32,56},{40,64},{48,72},{56,80},{64,... | collective-permute-start | bytes 393224 | tf_op jit(solution)/shard_map/ppermute | solution.py:15
  58.2 5.3 %collective-permute-start.8 = (bf16[512,128]{1,0:T(8,128)(2,1)S(1)}, bf16[512,128]{1,0:T(8,128)(2,1)S(1)}, u32[]{:S(2)}, u32[]{:S(2)}) collective-permute-start(bf16[512,128]{1,0:T(8,128)(2,1)S(1)} %bitcast.55), channel_id=1, source_target_pairs={{0,16},{8,24},{16,32},{24,40},{32,48},{40,56},{48,64},{56,72},{64,... | collective-permute-start | bytes 393224 | tf_op jit(solution)/shard_map/ppermute | solution.py:15
  63.5 3.4 %collective-permute-start.9 = (bf16[512,128]{1,0:T(8,128)(2,1)S(1)}, bf16[512,128]{1,0:T(8,128)(2,1)S(1)}, u32[]{:S(2)}, u32[]{:S(2)}) collective-permute-start(bf16[512,128]{1,0:T(8,128)(2,1)S(1)} %bitcast.56), channel_id=1, source_target_pairs={{0,8},{8,16},{16,24},{24,32},{32,40},{40,48},{48,56},{56,64},{64,7... | collective-permute-start | bytes 393224 | tf_op jit(solution)/shard_map/ppermute | solution.py:15
  67.5 4.9 %collective-permute-done.9 = bf16[512,128]{1,0:T(8,128)(2,1)S(1)} collective-permute-done((bf16[512,128]{1,0:T(8,128)(2,1)S(1)}, bf16[512,128]{1,0:T(8,128)(2,1)S(1)}, u32[]{:S(2)}, u32[]{:S(2)}) %collective-permute-start.9) | collective-permute-done | bytes 131104 | tf_op jit(solution)/shard_map/ppermute | solution.py:15
  72.5 53.4 %while.11 = (s32[]{:T(128)}, bf16[8,512,128]{2,1,0:T(8,128)(2,1)S(1)}, s32[8]{0:T(128)S(1)}, bf16[512,1024]{1,0:T(8,128)(2,1)S(1)}, bf16[3072,128]{1,0:T(8,128)(...) while((s32[]{:T(128)}, ...), condition=%wide.region_3.4_spmd.clone, body=%wide.region_0.3_spmd.clone.sunk | while | flops 822737920 | bytes 20751568 | solution.py:40
  73.8 3.3 %fusion.35 = (f32[512]{0:T(512)S(1)}, f32[512,3072]{1,0:T(8,128)S(1)}) fusion(bf16[3072,128]{1,0:T(8,128)(2,1)} %get-tuple-element.203, bf16[512,1024]{1,0:T(8,128)(2,1)S(1)} %get-tuple-element.202, s32[]{:T(128)S(6)} %select_n.19, pred[3072]{0:T(1024)(128)(4,1)S(1)} %get-tuple-element.209, s32[512]{0:T(512)S(1)} %get-tuple-element.207, ...), kind=kOutput, calls=%fused_computation.32.clone.1 | convolution fusion | flops 413662720 | bytes 7242756 | tf_op jit(solution)/shard_map/while/body/eval_jaxpr/dot_general | solution.py:26
  80.5 3.3 %fusion.35 = (f32[512]{0:T(512)S(1)}, f32[512,3072]{1,0:T(8,128)S(1)}) fusion(bf16[3072,128]{1,0:T(8,128)(2,1)} %get-tuple-element.203, bf16[512,1024]{1,0:T(8,128)(2,1)S(1)} %get-tuple-element.202, s32[]{:T(128)S(6)} %select_n.19, pred[3072]{0:T(1024)(128)(4,1)S(1)} %get-tuple-element.209, s32[512]{0:T(512)S(1)} %get-tuple-element.207, ...), kind=kOutput, calls=%fused_computation.32.clone.1 | convolution fusion | flops 413662720 | bytes 7242756 | tf_op jit(solution)/shard_map/while/body/eval_jaxpr/dot_general | solution.py:26
  87.1 3.3 %fusion.35 = (f32[512]{0:T(512)S(1)}, f32[512,3072]{1,0:T(8,128)S(1)}) fusion(bf16[3072,128]{1,0:T(8,128)(2,1)} %get-tuple-element.203, bf16[512,1024]{1,0:T(8,128)(2,1)S(1)} %get-tuple-element.202, s32[]{:T(128)S(6)} %select_n.19, pred[3072]{0:T(1024)(128)(4,1)S(1)} %get-tuple-element.209, s32[512]{0:T(512)S(1)} %get-tuple-element.207, ...), kind=kOutput, calls=%fused_computation.32.clone.1 | convolution fusion | flops 413662720 | bytes 7242756 | tf_op jit(solution)/shard_map/while/body/eval_jaxpr/dot_general | solution.py:26
  91.4 1.1 fusion.37
  93.8 3.3 %fusion.35 = (f32[512]{0:T(512)S(1)}, f32[512,3072]{1,0:T(8,128)S(1)}) fusion(bf16[3072,128]{1,0:T(8,128)(2,1)} %get-tuple-element.203, bf16[512,1024]{1,0:T(8,128)(2,1)S(1)} %get-tuple-element.202, s32[]{:T(128)S(6)} %select_n.19, pred[3072]{0:T(1024)(128)(4,1)S(1)} %get-tuple-element.209, s32[512]{0:T(512)S(1)} %get-tuple-element.207, ...), kind=kOutput, calls=%fused_computation.32.clone.1 | convolution fusion | flops 413662720 | bytes 7242756 | tf_op jit(solution)/shard_map/while/body/eval_jaxpr/dot_general | solution.py:26
  98.1 1.1 fusion.37
  100.5 3.3 %fusion.35 = (f32[512]{0:T(512)S(1)}, f32[512,3072]{1,0:T(8,128)S(1)}) fusion(bf16[3072,128]{1,0:T(8,128)(2,1)} %get-tuple-element.203, bf16[512,1024]{1,0:T(8,128)(2,1)S(1)} %get-tuple-element.202, s32[]{:T(128)S(6)} %select_n.19, pred[3072]{0:T(1024)(128)(4,1)S(1)} %get-tuple-element.209, s32[512]{0:T(512)S(1)} %get-tuple-element.207, ...), kind=kOutput, calls=%fused_computation.32.clone.1 | convolution fusion | flops 413662720 | bytes 7242756 | tf_op jit(solution)/shard_map/while/body/eval_jaxpr/dot_general | solution.py:26
  107.2 3.3 %fusion.35 = (f32[512]{0:T(512)S(1)}, f32[512,3072]{1,0:T(8,128)S(1)}) fusion(bf16[3072,128]{1,0:T(8,128)(2,1)} %get-tuple-element.203, bf16[512,1024]{1,0:T(8,128)(2,1)S(1)} %get-tuple-element.202, s32[]{:T(128)S(6)} %select_n.19, pred[3072]{0:T(1024)(128)(4,1)S(1)} %get-tuple-element.209, s32[512]{0:T(512)S(1)} %get-tuple-element.207, ...), kind=kOutput, calls=%fused_computation.32.clone.1 | convolution fusion | flops 413662720 | bytes 7242756 | tf_op jit(solution)/shard_map/while/body/eval_jaxpr/dot_general | solution.py:26
  111.5 1.1 fusion.37
  113.9 3.3 %fusion.35 = (f32[512]{0:T(512)S(1)}, f32[512,3072]{1,0:T(8,128)S(1)}) fusion(bf16[3072,128]{1,0:T(8,128)(2,1)} %get-tuple-element.203, bf16[512,1024]{1,0:T(8,128)(2,1)S(1)} %get-tuple-element.202, s32[]{:T(128)S(6)} %select_n.19, pred[3072]{0:T(1024)(128)(4,1)S(1)} %get-tuple-element.209, s32[512]{0:T(512)S(1)} %get-tuple-element.207, ...), kind=kOutput, calls=%fused_computation.32.clone.1 | convolution fusion | flops 413662720 | bytes 7242756 | tf_op jit(solution)/shard_map/while/body/eval_jaxpr/dot_general | solution.py:26
  118.2 1.1 fusion.37
  120.5 3.3 %fusion.35 = (f32[512]{0:T(512)S(1)}, f32[512,3072]{1,0:T(8,128)S(1)}) fusion(bf16[3072,128]{1,0:T(8,128)(2,1)} %get-tuple-element.203, bf16[512,1024]{1,0:T(8,128)(2,1)S(1)} %get-tuple-element.202, s32[]{:T(128)S(6)} %select_n.19, pred[3072]{0:T(1024)(128)(4,1)S(1)} %get-tuple-element.209, s32[512]{0:T(512)S(1)} %get-tuple-element.207, ...), kind=kOutput, calls=%fused_computation.32.clone.1 | convolution fusion | flops 413662720 | bytes 7242756 | tf_op jit(solution)/shard_map/while/body/eval_jaxpr/dot_general | solution.py:26
  124.9 1.1 fusion.37
  127.2 20.7 %all_to_all.76 = bf16[8,64,1024]{2,1,0:T(8,128)(2,1)S(1)} all-to-all(bf16[8,64,1024]{2,1,0:T(8,128)(2,1)S(1)} %all_to_all.68), channel_id=1, replica_groups=mesh['ctx'=64,'head'=8] {'head'}, dimensions={0} | all-to-all | bytes 2097152 | tf_op jit(solution)/shard_map/all_to_all | solution.py:77
  (56 shorter events, 22.1 us)
Async XLA Ops:
  0.0 0.9 copy-start
  1.6 10.6 %all-to-all-start.1 = ((bf16[64,8,128]{2,0,1:T(8,128)(2,1)}), bf16[64,8,128]{2,0,1:T(8,128)(2,1)S(1)}, u32[]{:S(2)}, u32[]{:S(2)}) async-start(bf16[64,8,128]{2,0,1:T(8,128)(2,1)} %copy_bitcast_fusion.2), calls=%async_computation.1 | async-start | bytes 262144 | tf_op jit(solution)/shard_map/all_to_all | solution.py:65
  12.2 27.5 %all-to-all-start.2 = ((bf16[64,8,128]{2,0,1:T(8,128)(2,1)}), bf16[64,8,128]{2,0,1:T(8,128)(2,1)S(1)}, u32[]{:S(2)}, u32[]{:S(2)}) async-start(bf16[64,8,128]{2,0,1:T(8,128)(2,1)} %copy_bitcast_fusion.1), calls=%async_computation.2 | async-start | bytes 262144 | tf_op jit(solution)/shard_map/all_to_all | solution.py:66
  15.6 28.9 %collective-permute-start = (bf16[512,128]{1,0:T(8,128)(2,1)S(1)}, bf16[512,128]{1,0:T(8,128)(2,1)S(1)}, u32[]{:S(2)}, u32[]{:S(2)}) collective-permute-start(bf16[512,128]{1,0:T(8,128)(2,1)S(1)} %bitcast.46), channel_id=1, source_target_pairs={{0,40},{8,48},{16,56},{24,64},{32,72},{40,80},{48,88},{56,96},{64,... | collective-permute-start | bytes 393224 | tf_op jit(solution)/shard_map/ppermute | solution.py:15
  20.4 29.8 %collective-permute-start.1 = (bf16[512,128]{1,0:T(8,128)(2,1)S(1)}, bf16[512,128]{1,0:T(8,128)(2,1)S(1)}, u32[]{:S(2)}, u32[]{:S(2)}) collective-permute-start(bf16[512,128]{1,0:T(8,128)(2,1)S(1)} %bitcast.47), channel_id=1, source_target_pairs={{0,32},{8,40},{16,48},{24,56},{32,64},{40,72},{48,80},{56,88},{64,... | collective-permute-start | bytes 393224 | tf_op jit(solution)/shard_map/ppermute | solution.py:15
  27.3 26.8 %collective-permute-start.2 = (bf16[512,128]{1,0:T(8,128)(2,1)S(1)}, bf16[512,128]{1,0:T(8,128)(2,1)S(1)}, u32[]{:S(2)}, u32[]{:S(2)}) collective-permute-start(bf16[512,128]{1,0:T(8,128)(2,1)S(1)} %bitcast.48), channel_id=1, source_target_pairs={{0,24},{8,32},{16,40},{24,48},{32,56},{40,64},{48,72},{56,80},{64,... | collective-permute-start | bytes 393224 | tf_op jit(solution)/shard_map/ppermute | solution.py:15
  33.5 24.7 %collective-permute-start.3 = (bf16[512,128]{1,0:T(8,128)(2,1)S(1)}, bf16[512,128]{1,0:T(8,128)(2,1)S(1)}, u32[]{:S(2)}, u32[]{:S(2)}) collective-permute-start(bf16[512,128]{1,0:T(8,128)(2,1)S(1)} %bitcast.49), channel_id=1, source_target_pairs={{0,16},{8,24},{16,32},{24,40},{32,48},{40,56},{48,64},{56,72},{64,... | collective-permute-start | bytes 393224 | tf_op jit(solution)/shard_map/ppermute | solution.py:15
  37.2 26.2 %collective-permute-start.4 = (bf16[512,128]{1,0:T(8,128)(2,1)S(1)}, bf16[512,128]{1,0:T(8,128)(2,1)S(1)}, u32[]{:S(2)}, u32[]{:S(2)}) collective-permute-start(bf16[512,128]{1,0:T(8,128)(2,1)S(1)} %bitcast.50), channel_id=1, source_target_pairs={{0,8},{8,16},{16,24},{24,32},{32,40},{40,48},{48,56},{56,64},{64,7... | collective-permute-start | bytes 393224 | tf_op jit(solution)/shard_map/ppermute | solution.py:15
  39.7 32.8 %all-to-all-start = ((bf16[64,8,1024]{2,0,1:T(8,128)(2,1)}), bf16[64,8,1024]{2,0,1:T(8,128)(2,1)S(1)}, u32[]{:S(2)}, u32[]{:S(2)}) async-start(bf16[64,8,1024]{2,0,1:T(8,128)(2,1)} %bitcast.33), calls=%async_computation | async-start | bytes 2097152 | tf_op jit(solution)/shard_map/all_to_all | solution.py:64
  44.4 22.5 %collective-permute-start.5 = (bf16[512,128]{1,0:T(8,128)(2,1)S(1)}, bf16[512,128]{1,0:T(8,128)(2,1)S(1)}, u32[]{:S(2)}, u32[]{:S(2)}) collective-permute-start(bf16[512,128]{1,0:T(8,128)(2,1)S(1)} %bitcast.52), channel_id=1, source_target_pairs={{0,40},{8,48},{16,56},{24,64},{32,72},{40,80},{48,88},{56,96},{64,... | collective-permute-start | bytes 393224 | tf_op jit(solution)/shard_map/ppermute | solution.py:15
  50.2 16.8 %collective-permute-start.6 = (bf16[512,128]{1,0:T(8,128)(2,1)S(1)}, bf16[512,128]{1,0:T(8,128)(2,1)S(1)}, u32[]{:S(2)}, u32[]{:S(2)}) collective-permute-start(bf16[512,128]{1,0:T(8,128)(2,1)S(1)} %bitcast.53), channel_id=1, source_target_pairs={{0,32},{8,40},{16,48},{24,56},{32,64},{40,72},{48,80},{56,88},{64,... | collective-permute-start | bytes 393224 | tf_op jit(solution)/shard_map/ppermute | solution.py:15
  54.1 13.0 %collective-permute-start.7 = (bf16[512,128]{1,0:T(8,128)(2,1)S(1)}, bf16[512,128]{1,0:T(8,128)(2,1)S(1)}, u32[]{:S(2)}, u32[]{:S(2)}) collective-permute-start(bf16[512,128]{1,0:T(8,128)(2,1)S(1)} %bitcast.54), channel_id=1, source_target_pairs={{0,24},{8,32},{16,40},{24,48},{32,56},{40,64},{48,72},{56,80},{64,... | collective-permute-start | bytes 393224 | tf_op jit(solution)/shard_map/ppermute | solution.py:15
  58.2 9.4 %collective-permute-start.8 = (bf16[512,128]{1,0:T(8,128)(2,1)S(1)}, bf16[512,128]{1,0:T(8,128)(2,1)S(1)}, u32[]{:S(2)}, u32[]{:S(2)}) collective-permute-start(bf16[512,128]{1,0:T(8,128)(2,1)S(1)} %bitcast.55), channel_id=1, source_target_pairs={{0,16},{8,24},{16,32},{24,40},{32,48},{40,56},{48,64},{56,72},{64,... | collective-permute-start | bytes 393224 | tf_op jit(solution)/shard_map/ppermute | solution.py:15
  63.5 9.0 %collective-permute-start.9 = (bf16[512,128]{1,0:T(8,128)(2,1)S(1)}, bf16[512,128]{1,0:T(8,128)(2,1)S(1)}, u32[]{:S(2)}, u32[]{:S(2)}) collective-permute-start(bf16[512,128]{1,0:T(8,128)(2,1)S(1)} %bitcast.56), channel_id=1, source_target_pairs={{0,8},{8,16},{16,24},{24,32},{32,40},{40,48},{48,56},{56,64},{64,7... | collective-permute-start | bytes 393224 | tf_op jit(solution)/shard_map/ppermute | solution.py:15
  66.9 5.5 %copy-start.1 = (bf16[3072,128]{1,0:T(8,128)(2,1)}, bf16[3072,128]{1,0:T(8,128)(2,1)S(1)}, u32[]{:S(2)}) copy-start(bf16[3072,128]{1,0:T(8,128)(2,1)S(1)} %constant_dynamic-update-slice_fusion) | copy-start | bytes 2359300
where the time goes:
time: 150 us; the launch traced here: 149 us
  starting transfers between devices  55.8 us (37%)
  matrix products  35.4 us (24%)
  blocking collectives  20.7 us (14%)
  local copies, waits for them, and re-layouts  13.4 us (9%)
  waiting for transfers between devices  9.15 us (6%)
  other arithmetic  8.79 us (6%)
  loops' own time  5.38 us (4%)
    ppermute x10, starting transfers between devices, passed_along(): lax.ppermute(value, axis, [(source, source + steps) for source in range(i...  43.3 us
    dot_general x8, matrix products, one_head(): lax.dot_general(query_head, key_rows, (((1,), (1,)), ((), ())), preferred...  26.4 us
    all_to_all x1, blocking collectives, body(): lax.all_to_all(local_out, 'head', split_axis=0, concat_axis=1, tiled=True)  20.7 us
    dot_general x8, matrix products, one_head(): jnp.dot(weights.astype(jnp.bfloat16), value_rows, preferred_element_type=...  8.96 us
    reduce_sum x8, other arithmetic, one_head(): totals = jnp.sum(weights, axis=1, keepdims=True)  7.97 us
    ppermute x10, waiting for transfers between devices, passed_along(): lax.ppermute(value, axis, [(source, source + steps) for source in range(i...  5.39 us
    another operation x1, loops' own time, attend(): stacked = lax.map(one_head, jnp.arange(query_heads, dtype=jnp.int32))  5.38 us
    dynamic_slice x8, local copies, waits for them, and re-layouts, attend(): stacked = lax.map(one_head, jnp.arange(query_heads, dtype=jnp.int32))  4.69 us
  transfers between devices with their start and end apart: 13, of which 3 were waited for; matrix products, arithmetic and copies ran while one was open for 4% of the time, Pallas kernels for 0%

commit v1 on v0

v1 whole, which is shorter than its diff:
```python
import math

import jax
import jax.numpy as jnp
from jax import lax
from jax.experimental import pallas as pl
from jax.experimental.pallas import tpu as pltpu
from jax.sharding import Mesh
from jax.sharding import PartitionSpec as P

HD = 128
GRAN = 256
BACK = 10
OWN = 8
HALF = GRAN // 2
HEADS = 2
AXES = ("z", "x", "y", "core")
FACTOR = math.log2(math.e) / math.sqrt(HD)
HIDDEN = -2.0e30


def kernel(
    plan, q_ref, seen_ref, qdoc_ref, own_m, own_o, prev_m, prev_o, tail_m, tail_o,
    o_ref, ks, vs, acc, peak, sems,
):
    tile = pl.program_id(0)

    @pl.when(tile == 0)
    def _():
        copies = []
        number = 0
        for first, count, pair in (
            (BACK, OWN, (own_m, own_o)),
            (BACK - OWN, OWN, (prev_m, prev_o)),
            (0, BACK - OWN, (tail_m, tail_o)),
        ):
            for half, src in enumerate(pair):
                there = (pl.ds(first, count), pl.ds(half * HALF, HALF))
                for part, dst in ((0, ks), (1, vs)):
                    copy = pltpu.make_async_copy(
                        src.at[:, :, pl.ds(part * HD, HD)],
                        dst.at[there[0], there[1], pl.ds(0, HD)],
                        sems.at[number],
                    )
                    copy.start()
                    copies.append(copy)
                    number += 1
        vs[:, :, HD:] = jnp.ones((BACK + OWN, GRAN, HD), jnp.bfloat16)
        for copy in copies:
            copy.wait()

    diagonal = BACK + tile
    low = plan[0, tile]
    full = plan[1, tile]

    def step(first, count, masked, fresh):
        keys = ks[pl.ds(first, count)].reshape(count * GRAN, HD)
        values = vs[pl.ds(first, count)].reshape(count * GRAN, 2 * HD)
        if masked:
            kdoc = jnp.concatenate([seen_ref[first + k, 0:1] for k in range(count)], axis=1)
            kpos = jnp.concatenate([seen_ref[first + k, 1:2] for k in range(count)], axis=1)
            qdoc = jnp.concatenate([qdoc_ref[...]] * (count * 2), axis=1)
            qpos = diagonal * GRAN + lax.broadcasted_iota(jnp.int32, (GRAN, count * GRAN), 0)
            visible = (qdoc == kdoc) & (kpos <= qpos)
        for head in range(HEADS):
            query = q_ref[:, head * HD:(head + 1) * HD]
            scores = lax.dot_general(
                query, keys, (((1,), (1,)), ((), ())), preferred_element_type=jnp.float32
            )
            if masked:
                scores = jnp.where(visible, scores, HIDDEN)
            top = jnp.max(scores, axis=1, keepdims=True)
            if not fresh:
                before = peak[head]
                top = jnp.maximum(before[:, :1], top)
            weights = jnp.exp2((scores - top) * FACTOR).astype(jnp.bfloat16)
            mixed = jnp.dot(weights, values, preferred_element_type=jnp.float32)
            if fresh:
                acc[head] = mixed
            else:
                shrink = jnp.exp2((before[:, :1] - top) * FACTOR)
                acc[head] = acc[head] * shrink + mixed
            peak[head] = jnp.broadcast_to(top, (GRAN, HD))

    step(diagonal, 1, True, True)
    ahead = diagonal - low
    odd = lax.rem(ahead, 2)

    @pl.when(odd == 1)
    def _():
        step(low, 1, True, False)

    def pairs(number, carry):
        first = low + odd + 2 * number

        @pl.when(first < full)
        def _():
            step(first, 2, True, False)

        @pl.when(first >= full)
        def _():
            step(first, 2, False, False)

        return carry

    lax.fori_loop(0, lax.div(ahead, 2), pairs, 0)
    for head in range(HEADS):
        whole = acc[head]
        o_ref[:, head * HD:(head + 1) * HD] = (whole[:, :HD] / whole[:, HD:]).astype(jnp.bfloat16)


def attend(plan, queries, seen, qdoc, pieces):
    window = BACK + OWN
    rows = OWN * GRAN
    return pl.pallas_call(
        kernel,
        grid_spec=pltpu.PrefetchScalarGridSpec(
            num_scalar_prefetch=1,
            grid=(OWN,),
            in_specs=[
                pl.BlockSpec((GRAN, HEADS * HD), lambda i, plan: (i, 0)),
                pl.BlockSpec((window, 2, GRAN), lambda i, plan: (0, 0, 0)),
                pl.BlockSpec((GRAN, HD), lambda i, plan: (i, 0)),
            ]
            + [pl.BlockSpec(memory_space=pl.ANY)] * 6,
            out_specs=pl.BlockSpec((GRAN, HEADS * HD), lambda i, plan: (i, 0)),
            scratch_shapes=[
                pltpu.VMEM((window, GRAN, HD), jnp.bfloat16),
                pltpu.VMEM((window, GRAN, 2 * HD), jnp.bfloat16),
                pltpu.VMEM((HEADS, GRAN, 2 * HD), jnp.float32),
                pltpu.VMEM((HEADS, GRAN, HD), jnp.float32),
                pltpu.SemaphoreType.DMA((12,)),
            ],
        ),
        out_shape=jax.ShapeDtypeStruct((rows, HEADS * HD), jnp.bfloat16),
        compiler_params=pltpu.CompilerParams(vmem_limit_bytes=24 * 1024 * 1024),
        cost_estimate=pl.CostEstimate(
            flops=4 * rows * HEADS * HD * 1536,
            bytes_accessed=6 * 1024 * 1024,
            transcendentals=rows * HEADS * 1536,
        ),
    )(plan, queries, seen, qdoc, *pieces)


def moved(value, sizes, there):
    zs, xs, ys, cores = sizes
    pairs = []
    for z in range(zs):
        for x in range(xs):
            for y in range(ys):
                for core in range(cores):
                    place = there(z, x, y, core)
                    if place is not None:
                        index = [((p[0] * xs + p[1]) * ys + p[2]) * cores + p[3] for p in ((z, x, y, core), place)]
                        pairs.append(tuple(index))
    return lax.ppermute(value, AXES, pairs)


def body(sizes, queries, keys, values, doc_ids):
    zs, xs, ys, cores = sizes
    chips = xs * ys
    teams = chips * cores
    tokens = queries.shape[0]
    key_heads = keys.shape[1] // HD
    plane = OWN * GRAN
    swap = lambda z, x, y, core: (z, x, y, 1 - core)

    both = jnp.stack([keys.reshape(tokens, key_heads, HD), values.reshape(tokens, key_heads, HD)], axis=2)
    both = jnp.transpose(both.reshape(tokens, key_heads, 2 * HD), (1, 0, 2))
    both = jnp.repeat(both, chips // key_heads, axis=0)
    own_m = lax.all_to_all(both, ("x", "y"), 0, 0, tiled=True).reshape(OWN, HALF, 2 * HD)
    prev_m = moved(own_m, sizes, lambda z, x, y, core: (z + 1, x, y, core) if z + 1 < zs else None)
    tail_m = moved(own_m[2 * OWN - BACK:], sizes, lambda z, x, y, core: (z + 2, x, y, core) if z + 2 < zs else None)
    own_o = moved(own_m, sizes, swap)
    prev_o = moved(prev_m, sizes, swap)
    tail_o = moved(tail_m, sizes, swap)

    wide = jnp.transpose(queries.reshape(tokens, teams, HEADS * HD), (1, 0, 2))
    local = lax.all_to_all(wide, ("x", "y", "core"), 0, 0, tiled=True).reshape(plane, HEADS * HD)

    first = lax.axis_index("z") * plane
    padded = jnp.concatenate([jnp.full((BACK * GRAN,), -1, jnp.int32), doc_ids])
    window = lax.dynamic_slice_in_dim(padded, first, (BACK + OWN) * GRAN, 0)
    place = jnp.arange((BACK + OWN) * GRAN, dtype=jnp.int32)
    qids = window[BACK * GRAN:]
    starts = jnp.sum(
        window[None, None, :] < jnp.stack([qids[::GRAN], qids[GRAN - 1::GRAN]])[:, :, None],
        axis=2, dtype=jnp.int32,
    )
    plan = jnp.stack([starts[0] // GRAN, (starts[1] + GRAN - 1) // GRAN])
    core = lax.axis_index("core")

    def by_holder(line):
        split = jnp.transpose(line.reshape(BACK + OWN, GRAN // (cores * tokens), cores, tokens), (0, 2, 1, 3))
        split = split.reshape(BACK + OWN, cores, HALF)
        return jnp.where(core == 0, split, split[:, ::-1]).reshape(BACK + OWN, GRAN)

    seen = jnp.stack([by_holder(window), by_holder(place)], axis=1)
    qdoc = jnp.broadcast_to(qids[:, None], (plane, HD))

    out = attend(plan, local, seen, qdoc, (own_m, own_o, prev_m, prev_o, tail_m, tail_o))
    back = lax.all_to_all(out.reshape(teams, tokens, HEADS * HD), ("x", "y", "core"), 0, 0, tiled=True)
    return jnp.transpose(back, (1, 0, 2)).reshape(tokens, teams * HEADS * HD)


def solution(mesh):
    sizes = (16, 4, 4, 2)
    grid = Mesh(mesh.devices.reshape(sizes), AXES)

    def run(*args):
        return body(sizes, *args)

    return jax.shard_map(
        run,
        mesh=grid,
        in_specs=(P(AXES, None), P(AXES, None), P(AXES, None), P()),
        out_specs=P(AXES, None),
        check_vma=False,
    )
```

time: 150 us -> 116 us (0.77)
  the two profiles are of different devices: /device:TPU:32 before, /device:TPU:129 now
where the time goes in v1:
time: 116 us; the launch traced here: 115 us
  Pallas kernels  29.8 us (26%)
  starting transfers between devices  27.8 us (24%)
  waiting for transfers between devices  27.4 us (24%)
  blocking collectives  24.2 us (21%)
  local copies, waits for them, and re-layouts  5.2 us (4%)
    pallas_call x1, Pallas kernels, attend(): pl.pallas_call(kernel, grid_spec=pltpu.PrefetchScalarGridSpec(num_scalar_...  29.8 us
    all_to_all x1, blocking collectives, body(): lax.all_to_all(out.reshape(teams, tokens, HEADS * HD), ('x', 'y', 'core')...  24.2 us
    ppermute x5, waiting for transfers between devices, moved(): return lax.ppermute(value, AXES, pairs)  18.4 us
    ppermute x5, starting transfers between devices, moved(): return lax.ppermute(value, AXES, pairs)  15.2 us
    all_to_all x1, waiting for transfers between devices, body(): lax.all_to_all(both, ('x', 'y'), 0, 0, tiled=True)  8.99 us
    all_to_all x1, starting transfers between devices, body(): lax.all_to_all(both, ('x', 'y'), 0, 0, tiled=True)  6.75 us
    all_to_all x1, starting transfers between devices, body(): lax.all_to_all(wide, ('x', 'y', 'core'), 0, 0, tiled=True)  5.86 us
  transfers between devices with their start and end apart: 7, of which 4 were waited for; matrix products, arithmetic and copies ran while one was open for 2% of the time, Pallas kernels for 0%

profile of v1, /device:TPU:129, one launch (start us, length us, event | category | flops | bytes accessed | tf_op | source)
XLA Modules:
  0.0 115.0 jit_solution(15450061952104175323)
XLA Ops:
  0.0 1.0 copy.21
  1.1 0.0 copy-start
  1.1 0.8 broadcast_in_dim.5
  2.0 6.8 %all-to-all-start.1 = ((bf16[16,64,256]{2,1,0:T(8,128)(2,1)}), bf16[16,64,256]{2,1,0:T(8,128)(2,1)S(1)}, u32[]{:S(2)}, u32[]{:S(2)}) async-start(bf16[16,64,256]{2,1,0:T(8,128)(2,1)} %bitcast.9), calls=%async_computation.1 | async-start | bytes 1048576 | tf_op jit(solution)/shard_map/all_to_all | solution.py:171
  8.8 1.1 copy.23
  9.9 0.1 reshape.82
  9.9 0.1 iota.44
  10.0 9.0 %all-to-all-done.1 = bf16[16,64,256]{2,1,0:T(8,128)(2,1)S(1)} async-done(((bf16[16,64,256]{2,1,0:T(8,128)(2,1)}), bf16[16,64,256]{2,1,0:T(8,128)(2,1)S(1)}, u32[]{:S(2)}, u32[]{:S(2)}) %all-to-all-start.1) | async-done | bytes 524320 | tf_op jit(solution)/shard_map/all_to_all | solution.py:171
  19.0 5.9 %all-to-all-start = ((bf16[32,64,256]{2,1,0:T(8,128)(2,1)}), bf16[32,64,256]{2,1,0:T(8,128)(2,1)S(1)}, u32[]{:S(2)}, u32[]{:S(2)}) async-start(bf16[32,64,256]{2,1,0:T(8,128)(2,1)} %bitcast.31), calls=%async_computation | async-start | bytes 2097152 | tf_op jit(solution)/shard_map/all_to_all | solution.py:179
  24.9 3.5 %collective-permute-start.1 = (bf16[8,128,256]{2,1,0:T(8,128)(2,1)S(1)}, bf16[8,128,256]{2,1,0:T(8,128)(2,1)S(1)}, u32[]{:S(2)}, u32[]{:S(2)}) collective-permute-start(bf16[8,128,256]{2,1,0:T(8,128)(2,1)S(1)} %bitcast.34), channel_id=1, source_target_pairs={{0,32},{1,33},{2,34},{3,35},{4,36},{5,37},{6,38},{7,39},{8,40},{9,... | collective-permute-start | bytes 1572872 | tf_op jit(solution)/shard_map/ppermute | solution.py:156
  28.5 0.1 pad_dynamic-slice_fusion
  28.6 0.1 slice.23
  28.7 0.1 slice.22
  28.7 0.1 rev.7
  28.8 0.1 pad_dynamic-slice_fusion.1
  28.9 0.1 reshape.75
  29.0 0.1 reshape.76
  29.2 2.5 %collective-permute-start = (bf16[8,128,256]{2,1,0:T(8,128)(2,1)S(1)}, bf16[8,128,256]{2,1,0:T(8,128)(2,1)S(1)}, u32[]{:S(2)}, u32[]{:S(2)}) collective-permute-start(bf16[8,128,256]{2,1,0:T(8,128)(2,1)S(1)} %bitcast.35), channel_id=1, source_target_pairs={{0,1},{1,0},{2,3},{3,2},{4,5},{5,4},{6,7},{7,6},{8,9},{9,8},{10,11... | collective-permute-start | bytes 1572872 | tf_op jit(solution)/shard_map/ppermute | solution.py:156
  31.8 9.4 %collective-permute-done.1.prev_m = bf16[8,128,256]{2,1,0:T(8,128)(2,1)S(1)} collective-permute-done((bf16[8,128,256]{2,1,0:T(8,128)(2,1)S(1)}, bf16[8,128,256]{2,1,0:T(8,128)(2,1)S(1)}, u32[]{:S(2)}, u32[]{:S(2)}) %collective-permute-start.1) | collective-permute-done | bytes 524320 | tf_op jit(solution)/shard_map/ppermute | solution.py:156
  41.2 3.1 %collective-permute-start.2 = (bf16[8,128,256]{2,1,0:T(8,128)(2,1)S(1)}, bf16[8,128,256]{2,1,0:T(8,128)(2,1)S(1)}, u32[]{:S(2)}, u32[]{:S(2)}) collective-permute-start(bf16[8,128,256]{2,1,0:T(8,128)(2,1)S(1)} %collective-permute-done.1.prev_m), channel_id=1, source_target_pairs={{0,1},{1,0},{2,3},{3,2},{4,5},{5,4},{6,7},{7,6},{8,9},{9,8},{10,11... | collective-permute-start | bytes 1572872 | tf_op jit(solution)/shard_map/ppermute | solution.py:156
  44.3 0.2 convert_reduce_fusion
  44.5 3.7 %collective-permute-start.3 = (bf16[2,128,256]{2,1,0:T(8,128)(2,1)S(1)}, bf16[2,128,256]{2,1,0:T(8,128)(2,1)S(1)}, u32[]{:S(2)}, u32[]{:S(2)}) collective-permute-start(bf16[2,128,256]{2,1,0:T(8,128)(2,1)S(1)} %bitcast.44), channel_id=1, source_target_pairs={{0,64},{1,65},{2,66},{3,67},{4,68},{5,69},{6,70},{7,71},{8,72},{9,... | collective-permute-start | bytes 393224 | tf_op jit(solution)/shard_map/ppermute | solution.py:156
  48.2 8.0 %collective-permute-done.3.tail_m = bf16[2,128,256]{2,1,0:T(8,128)(2,1)S(1)} collective-permute-done((bf16[2,128,256]{2,1,0:T(8,128)(2,1)S(1)}, bf16[2,128,256]{2,1,0:T(8,128)(2,1)S(1)}, u32[]{:S(2)}, u32[]{:S(2)}) %collective-permute-start.3) | collective-permute-done | bytes 131104 | tf_op jit(solution)/shard_map/ppermute | solution.py:156
  56.3 2.3 %collective-permute-start.4 = (bf16[2,128,256]{2,1,0:T(8,128)(2,1)S(1)}, bf16[2,128,256]{2,1,0:T(8,128)(2,1)S(1)}, u32[]{:S(2)}, u32[]{:S(2)}) collective-permute-start(bf16[2,128,256]{2,1,0:T(8,128)(2,1)S(1)} %collective-permute-done.3.tail_m), channel_id=1, source_target_pairs={{0,1},{1,0},{2,3},{3,2},{4,5},{5,4},{6,7},{7,6},{8,9},{9,8},{10,11... | collective-permute-start | bytes 393224 | tf_op jit(solution)/shard_map/ppermute | solution.py:156
  58.7 0.9 collective-permute-done.4.tail_o
  59.6 0.0 all-to-all-done
  59.6 0.0 collective-permute-done.own_o
  59.6 0.0 collective-permute-done.2.prev_o
  59.6 0.3 broadcast_in_dim.4.qdoc_ref
  59.9 29.8 %shard_map.46 = bf16[2048,256]{1,0:T(8,128)(2,1)S(1)} custom-call(s32[2,8]{1,0:T(2,128)S(1)} %pad_add_fusion.2.plan, bf16[2048,256]{1,0:T(8,128)(2,1)S(1)} %bitcast.32, s32[18,2,256]{2,1,0:T(2,128)S(1)} %pad_add_fusion.seen_ref, s32[2048,128]{1,0:T(8,128)S(1)} %broadcast_in_dim.4.qdoc_ref, bf16[8,128,256]{2,1,0:T(8,128)(2,1)S(1)} %bitcast.36, ...), custom_call_target="tpu_custom_call" | custom-call | flops 3221225472 | bytes 6291456 | tf_op jit(solution)/shard_map/pallas_call | solution.py:115
  89.8 24.2 %all_to_all.15 = bf16[32,64,256]{2,1,0:T(8,128)(2,1)S(1)} all-to-all(bf16[32,64,256]{2,1,0:T(8,128)(2,1)S(1)} %bitcast.33), channel_id=1, replica_groups=mesh['z'=16,'x'=4,'y'=4,'core'=2] {'x','y','core'}, dimensions={0} | all-to-all | bytes 2097152 | tf_op jit(solution)/shard_map/all_to_all | solution.py:202
  114.0 1.0 copy.19
  (19 shorter events, 0.3 us)
Async XLA Ops:
  0.0 1.0 copy-start.2
  1.1 7.6 %copy-start = (bf16[64,8192]{1,0:T(8,128)(2,1)S(1)}, bf16[64,8192]{1,0:T(8,128)(2,1)}, u32[]{:S(2)}) copy-start(bf16[64,8192]{1,0:T(8,128)(2,1)} %param.4) | copy-start | bytes 3145732
  2.0 17.1 %all-to-all-start.1 = ((bf16[16,64,256]{2,1,0:T(8,128)(2,1)}), bf16[16,64,256]{2,1,0:T(8,128)(2,1)S(1)}, u32[]{:S(2)}, u32[]{:S(2)}) async-start(bf16[16,64,256]{2,1,0:T(8,128)(2,1)} %bitcast.9), calls=%async_computation.1 | async-start | bytes 1048576 | tf_op jit(solution)/shard_map/all_to_all | solution.py:171
  19.0 9.4 %copy-start.1 = (s32[32768]{0:T(1024)S(1)}, s32[32768]{0:T(1024)}, u32[]{:S(2)}) copy-start(s32[32768]{0:T(1024)} %param.7) | copy-start | bytes 393220
  19.0 40.6 %all-to-all-start = ((bf16[32,64,256]{2,1,0:T(8,128)(2,1)}), bf16[32,64,256]{2,1,0:T(8,128)(2,1)S(1)}, u32[]{:S(2)}, u32[]{:S(2)}) async-start(bf16[32,64,256]{2,1,0:T(8,128)(2,1)} %bitcast.31), calls=%async_computation | async-start | bytes 2097152 | tf_op jit(solution)/shard_map/all_to_all | solution.py:179
  24.9 16.3 %collective-permute-start.1 = (bf16[8,128,256]{2,1,0:T(8,128)(2,1)S(1)}, bf16[8,128,256]{2,1,0:T(8,128)(2,1)S(1)}, u32[]{:S(2)}, u32[]{:S(2)}) collective-permute-start(bf16[8,128,256]{2,1,0:T(8,128)(2,1)S(1)} %bitcast.34), channel_id=1, source_target_pairs={{0,32},{1,33},{2,34},{3,35},{4,36},{5,37},{6,38},{7,39},{8,40},{9,... | collective-permute-start | bytes 1572872 | tf_op jit(solution)/shard_map/ppermute | solution.py:156
  29.2 30.4 %collective-permute-start = (bf16[8,128,256]{2,1,0:T(8,128)(2,1)S(1)}, bf16[8,128,256]{2,1,0:T(8,128)(2,1)S(1)}, u32[]{:S(2)}, u32[]{:S(2)}) collective-permute-start(bf16[8,128,256]{2,1,0:T(8,128)(2,1)S(1)} %bitcast.35), channel_id=1, source_target_pairs={{0,1},{1,0},{2,3},{3,2},{4,5},{5,4},{6,7},{7,6},{8,9},{9,8},{10,11... | collective-permute-start | bytes 1572872 | tf_op jit(solution)/shard_map/ppermute | solution.py:156
  41.2 18.4 %collective-permute-start.2 = (bf16[8,128,256]{2,1,0:T(8,128)(2,1)S(1)}, bf16[8,128,256]{2,1,0:T(8,128)(2,1)S(1)}, u32[]{:S(2)}, u32[]{:S(2)}) collective-permute-start(bf16[8,128,256]{2,1,0:T(8,128)(2,1)S(1)} %collective-permute-done.1.prev_m), channel_id=1, source_target_pairs={{0,1},{1,0},{2,3},{3,2},{4,5},{5,4},{6,7},{7,6},{8,9},{9,8},{10,11... | collective-permute-start | bytes 1572872 | tf_op jit(solution)/shard_map/ppermute | solution.py:156
  44.5 11.8 %collective-permute-start.3 = (bf16[2,128,256]{2,1,0:T(8,128)(2,1)S(1)}, bf16[2,128,256]{2,1,0:T(8,128)(2,1)S(1)}, u32[]{:S(2)}, u32[]{:S(2)}) collective-permute-start(bf16[2,128,256]{2,1,0:T(8,128)(2,1)S(1)} %bitcast.44), channel_id=1, source_target_pairs={{0,64},{1,65},{2,66},{3,67},{4,68},{5,69},{6,70},{7,71},{8,72},{9,... | collective-permute-start | bytes 393224 | tf_op jit(solution)/shard_map/ppermute | solution.py:156
  56.3 3.3 %collective-permute-start.4 = (bf16[2,128,256]{2,1,0:T(8,128)(2,1)S(1)}, bf16[2,128,256]{2,1,0:T(8,128)(2,1)S(1)}, u32[]{:S(2)}, u32[]{:S(2)}) collective-permute-start(bf16[2,128,256]{2,1,0:T(8,128)(2,1)S(1)} %collective-permute-done.3.tail_m), channel_id=1, source_target_pairs={{0,1},{1,0},{2,3},{3,2},{4,5},{5,4},{6,7},{7,6},{8,9},{9,8},{10,11... | collective-permute-start | bytes 393224 | tf_op jit(solution)/shard_map/ppermute | solution.py:156

commit v2 on v0

v2 whole, which is shorter than its diff:
```python
import math

import jax
import jax.numpy as jnp
from jax import lax
from jax.experimental import pallas as pl
from jax.experimental.pallas import tpu as pltpu
from jax.sharding import Mesh
from jax.sharding import PartitionSpec as P

HD = 128
GRAN = 256
BACK = 10
OWN = 8
SPAN = 4
PAD = SPAN - 1
HALF = GRAN // 2
CHUNK = 64
HEADS = 2
COLS = HEADS * GRAN
ONES = 16
AXES = ("z", "x", "y", "core")
FACTOR = math.log2(math.e) / math.sqrt(HD)
HIDDEN = -2.0e30
FAR = 1 << 20
VMEM = pltpu.VMEM


def work(items, info, starts_ref, causal, ks, vt, qt, spot, acc, peak, sa, sb):
    def scored(number, buffer):
        tile, first = items[0, number], items[1, number]
        keys = ks[pl.ds(first, SPAN)].reshape(SPAN * GRAN, 2 * HD)
        raw = jnp.dot(keys, qt[tile], preferred_element_type=jnp.float32)
        low = starts_ref[tile] - (first - PAD) * GRAN + items[2, number]
        place = jnp.concatenate([spot[...]] * (COLS // HD), axis=1)
        best = None
        for k in range(SPAN):
            rows = slice(k * GRAN, (k + 1) * GRAN)
            seen = place >= jnp.concatenate([low - k * GRAN] * HEADS, axis=1)
            if causal and k == SPAN - 1:
                own = (tile - first) * GRAN + lax.broadcasted_iota(jnp.int32, (1, GRAN), 1)
                seen = seen & (place <= jnp.concatenate([own] * HEADS, axis=1))
            piece = jnp.where(seen, raw[rows], HIDDEN)
            buffer[rows] = piece
            most = jnp.max(piece.reshape(GRAN // 8, 8, COLS), axis=0)
            best = most if best is None else jnp.maximum(best, most)
        return jnp.max(best, axis=0, keepdims=True)

    def finish(number, buffer, best):
        tile, first = items[0, number], items[1, number]
        before = peak[tile]
        top = jnp.maximum(before, best)
        peak[tile] = top
        weights = jnp.exp2(buffer[...] - top).astype(jnp.bfloat16)
        values = vt[:, pl.ds(pl.multiple_of(first * GRAN, GRAN), SPAN * GRAN)]
        mixed = jnp.dot(values, weights, preferred_element_type=jnp.float32)
        acc[tile] = acc[tile] * jnp.exp2(before - top) + mixed

    def both(pair, best):
        following = scored(2 * pair + 1, sb)
        finish(2 * pair, sa, best)
        best = scored(2 * pair + 2, sa)
        finish(2 * pair + 1, sb, following)
        return best

    lax.fori_loop(0, info[0], both, scored(0, sa))


def fill(info, groups, ks, vt, stage, spot, sems):
    copies = []
    for first, count, pair in groups:
        for half, source in enumerate(pair):
            rows = pl.ds(half * HALF, HALF)
            for part, there in (
                (0, ks.at[pl.ds(PAD + first, count), rows, pl.ds(0, HD)]),
                (0, ks.at[pl.ds(PAD + first, count), rows, pl.ds(HD, HD)]),
                (1, stage.at[pl.ds(first, count), rows, :]),
            ):
                copy = pltpu.make_async_copy(
                    source.at[:, :, pl.ds(part * HD, HD)], there, sems.at[len(copies)]
                )
                copy.start()
                copies.append(copy)
    granules = stage.shape[0]
    ks[:PAD] = jnp.zeros((PAD, GRAN, 2 * HD), jnp.bfloat16)
    vt[:, :PAD * GRAN] = jnp.zeros((HD + ONES, PAD * GRAN), jnp.bfloat16)
    vt[HD:, PAD * GRAN:] = jnp.ones((ONES, granules * GRAN), jnp.bfloat16)
    row = lax.broadcasted_iota(jnp.int32, (GRAN, HD), 0)
    holder = jnp.where(info[1] == 0, row // HALF, 1 - row // HALF)
    inner = row % HALF
    spot[...] = (inner // CHUNK) * (2 * CHUNK) + holder * CHUNK + inner % CHUNK
    return copies


def turn(granules, vt, stage):
    for g in range(granules):
        vt[:HD, (PAD + g) * GRAN:(PAD + g + 1) * GRAN] = stage[g].T


def own_kernel(items, info, q_ref, starts_ref, own_m, own_o, qt, acc, peak, ks, vt, stage, spot, sa, sb, sems):
    copies = fill(info, ((0, OWN, (own_m, own_o)),), ks, vt, stage, spot, sems)
    acc[...] = jnp.zeros_like(acc)
    peak[...] = jnp.full_like(peak, HIDDEN)
    for tile in range(OWN):
        for head in range(HEADS):
            cols = slice(head * GRAN, (head + 1) * GRAN)
            query = q_ref[tile * GRAN:(tile + 1) * GRAN, head * HD:(head + 1) * HD].T.astype(jnp.float32) * FACTOR
            coarse = query.astype(jnp.bfloat16)
            qt[tile, :HD, cols] = coarse
            qt[tile, HD:, cols] = (query - coarse.astype(jnp.float32)).astype(jnp.bfloat16)
    for copy in copies:
        copy.wait()
    turn(OWN, vt, stage)
    work(items, info, starts_ref, True, ks, vt, qt, spot, acc, peak, sa, sb)


def back_kernel(
    items, info, starts_ref, qt, acc_in, peak_in, prev_m, prev_o, tail_m, tail_o,
    o_ref, acc, peak, ks, vt, stage, spot, sa, sb, sems,
):
    tail = BACK - OWN
    copies = fill(info, ((tail, OWN, (prev_m, prev_o)), (0, tail, (tail_m, tail_o))), ks, vt, stage, spot, sems)
    acc[...] = acc_in[...]
    peak[...] = peak_in[...]
    for copy in copies:
        copy.wait()
    turn(BACK, vt, stage)
    work(items, info, starts_ref, False, ks, vt, qt, spot, acc, peak, sa, sb)
    for tile in range(OWN):
        for head in range(HEADS):
            cols = slice(head * GRAN, (head + 1) * GRAN)
            o_ref[tile * GRAN:(tile + 1) * GRAN, head * HD:(head + 1) * HD] = (
                (acc[tile, :HD, cols] / acc[tile, HD:HD + 1, cols]).T.astype(jnp.bfloat16)
            )


def scratch(granules, copies):
    return [
        VMEM((PAD + granules, GRAN, 2 * HD), jnp.bfloat16),
        VMEM((HD + ONES, (PAD + granules) * GRAN), jnp.bfloat16),
        VMEM((granules, GRAN, HD), jnp.bfloat16),
        VMEM((GRAN, HD), jnp.int32),
        VMEM((SPAN * GRAN, COLS), jnp.float32),
        VMEM((SPAN * GRAN, COLS), jnp.float32),
        pltpu.SemaphoreType.DMA((copies,)),
    ]


STATE = ((OWN, HD + ONES, COLS), jnp.float32), ((OWN, 1, COLS), jnp.float32)
LIMIT = pltpu.CompilerParams(vmem_limit_bytes=40 * 1024 * 1024)
INSIDE = pl.BlockSpec(memory_space=VMEM)
ANYWHERE = pl.BlockSpec(memory_space=pl.ANY)


def attend_own(items, info, queries, starts, pair):
    shapes = (((OWN, 2 * HD, COLS), jnp.bfloat16),) + STATE
    return pl.pallas_call(
        own_kernel,
        grid_spec=pltpu.PrefetchScalarGridSpec(
            num_scalar_prefetch=2,
            grid=(),
            in_specs=[INSIDE, INSIDE, ANYWHERE, ANYWHERE],
            out_specs=[INSIDE] * 3,
            scratch_shapes=scratch(OWN, 6),
        ),
        out_shape=[jax.ShapeDtypeStruct(*s) for s in shapes],
        compiler_params=LIMIT,
        cost_estimate=pl.CostEstimate(flops=10**6, bytes_accessed=8 << 20, transcendentals=0),
    )(items, info, queries, starts, *pair)


def attend_back(items, info, starts, state, pieces):
    return pl.pallas_call(
        back_kernel,
        grid_spec=pltpu.PrefetchScalarGridSpec(
            num_scalar_prefetch=2,
            grid=(),
            in_specs=[INSIDE] * 4 + [ANYWHERE] * 4,
            out_specs=INSIDE,
            scratch_shapes=[VMEM(*s) for s in STATE] + scratch(BACK, 12),
        ),
        out_shape=jax.ShapeDtypeStruct((OWN * GRAN, HEADS * HD), jnp.bfloat16),
        compiler_params=LIMIT,
        cost_estimate=pl.CostEstimate(flops=8 * 10**9, bytes_accessed=8 << 20, transcendentals=0),
    )(items, info, starts, *state, *pieces)


def agenda(counts, tops, room, core):
    tiles = jnp.arange(OWN, dtype=jnp.int32)
    ends = jnp.sum(jnp.where(tiles[None, :] <= tiles[:, None], counts[None, :], 0), axis=1)
    number = jnp.arange(room, dtype=jnp.int32)
    tile = jnp.minimum(jnp.sum(number[:, None] >= ends[None, :], axis=1, dtype=jnp.int32), OWN - 1)
    real = number < ends[-1]
    chosen = tile[:, None] == tiles[None, :]
    begin = jnp.sum(jnp.where(chosen, (ends - counts)[None, :], 0), axis=1)
    top = jnp.sum(jnp.where(chosen, tops[None, :], 0), axis=1)
    first = top - SPAN * jnp.where(real, number - begin, 0)
    items = jnp.stack([tile, first, jnp.where(real, 0, FAR)])
    return items, jnp.stack([(ends[-1] + 1) // 2, core])


def plans(doc_ids, first, core):
    plane = OWN * GRAN
    padded = jnp.concatenate([jnp.full((BACK * GRAN,), -1, jnp.int32), doc_ids])
    window = lax.dynamic_slice_in_dim(padded, first, (BACK + OWN) * GRAN, 0)
    ids = window[BACK * GRAN:]
    starts = jnp.sum(window[None, :] < ids[:, None], axis=1, dtype=jnp.int32)
    lows = starts[::GRAN] // GRAN
    tiles = jnp.arange(OWN, dtype=jnp.int32)
    mine = agenda((tiles - jnp.maximum(lows - BACK, 0)) // SPAN + 1, tiles, 16, core)
    older = agenda((jnp.maximum(BACK - lows, 0) + SPAN - 1) // SPAN, jnp.full((OWN,), BACK - 1, jnp.int32), 32, core)
    starts = starts.reshape(OWN, 1, GRAN)
    return mine, older, jnp.maximum(starts - BACK * GRAN, 0), starts


def moved(value, sizes, there):
    zs, xs, ys, cores = sizes
    pairs = []
    for z in range(zs):
        for x in range(xs):
            for y in range(ys):
                for core in range(cores):
                    place = there(z, x, y, core)
                    if place is not None:
                        index = [((p[0] * xs + p[1]) * ys + p[2]) * cores + p[3] for p in ((z, x, y, core), place)]
                        pairs.append(tuple(index))
    return lax.ppermute(value, AXES, pairs)


def body(sizes, queries, keys, values, doc_ids):
    zs, xs, ys, cores = sizes
    chips = xs * ys
    teams = chips * cores
    tokens = queries.shape[0]
    key_heads = keys.shape[1] // HD
    plane = OWN * GRAN

    def swap(value):
        return moved(value, sizes, lambda z, x, y, core: (z, x, y, 1 - core))

    def later(value, planes):
        return moved(value, sizes, lambda z, x, y, core: (z + planes, x, y, core) if z + planes < zs else None)

    both = jnp.stack([keys.reshape(tokens, key_heads, HD), values.reshape(tokens, key_heads, HD)], axis=2)
    both = jnp.transpose(both.reshape(tokens, key_heads, 2 * HD), (1, 0, 2))
    both = jnp.repeat(both, chips // key_heads, axis=0)
    own_m = lax.all_to_all(both, ("x", "y"), 0, 0, tiled=True).reshape(OWN, HALF, 2 * HD)
    prev_m = later(own_m, 1)
    tail_m = later(own_m[2 * OWN - BACK:], 2)
    prev_m, tail_m = lax.optimization_barrier((prev_m, tail_m))
    own_o = swap(own_m)
    prev_o = swap(prev_m)
    tail_o = swap(tail_m)

    wide = jnp.transpose(queries.reshape(tokens, teams, HEADS * HD), (1, 0, 2))
    wide, _ = lax.optimization_barrier((wide, own_m))
    local = lax.all_to_all(wide, ("x", "y", "core"), 0, 0, tiled=True).reshape(plane, HEADS * HD)

    mine, older, near, far = plans(doc_ids, lax.axis_index("z") * plane, lax.axis_index("core"))
    state = attend_own(*mine, local, near, (own_m, own_o))
    out = attend_back(*older, far, state, (prev_m, prev_o, tail_m, tail_o))
    back = lax.all_to_all(out.reshape(teams, tokens, HEADS * HD), ("x", "y", "core"), 0, 0, tiled=True)
    return jnp.transpose(back, (1, 0, 2)).reshape(tokens, teams * HEADS * HD)


def solution(mesh):
    sizes = (16, 4, 4, 2)
    grid = Mesh(mesh.devices.reshape(sizes), AXES)

    def run(*args):
        return body(sizes, *args)

    return jax.shard_map(
        run,
        mesh=grid,
        in_specs=(P(AXES, None), P(AXES, None), P(AXES, None), P()),
        out_specs=P(AXES, None),
        check_vma=False,
    )
```

time: 150 us -> 90.6 us (0.60)
  the two profiles are of different devices: /device:TPU:32 before, /device:TPU:129 now
where the time goes in v2:
time: 90.6 us; the launch traced here: 90.1 us
  starting transfers between devices  28.7 us (32%)
  blocking collectives  24.3 us (27%)
  Pallas kernels  17.5 us (19%)
  local copies, waits for them, and re-layouts  6.58 us (7%)
  other arithmetic  6.07 us (7%)
  waiting for transfers between devices  5.22 us (6%)
  between operations  1.62 us (2%)
    all_to_all x1, blocking collectives, body(): lax.all_to_all(out.reshape(teams, tokens, HEADS * HD), ('x', 'y', 'core')...  24.3 us
    ppermute x5, starting transfers between devices, moved(): return lax.ppermute(value, AXES, pairs)  16 us
    pallas_call x1, Pallas kernels, attend_own(): pl.pallas_call(own_kernel, grid_spec=pltpu.PrefetchScalarGridSpec(num_sca...  8.79 us
    pallas_call x1, Pallas kernels, attend_back(): pl.pallas_call(back_kernel, grid_spec=pltpu.PrefetchScalarGridSpec(num_sc...  8.74 us
    all_to_all x1, starting transfers between devices, body(): lax.all_to_all(both, ('x', 'y'), 0, 0, tiled=True)  6.75 us
    all_to_all x1, starting transfers between devices, body(): lax.all_to_all(wide, ('x', 'y', 'core'), 0, 0, tiled=True)  6.02 us
    reduce_sum x1, other arithmetic, plans(): starts = jnp.sum(window[None, :] < ids[:, None], axis=1, dtype=jnp.int32)  3.81 us
    all_to_all x1, waiting for transfers between devices, body(): lax.all_to_all(both, ('x', 'y'), 0, 0, tiled=True)  3.18 us
  transfers between devices with their start and end apart: 7, of which 2 were waited for; matrix products, arithmetic and copies ran while one was open for 10% of the time, Pallas kernels for 10%

profile of v2, /device:TPU:129, one launch (start us, length us, event | category | flops | bytes accessed | tf_op | source)
XLA Modules:
  0.0 90.1 jit_solution(9938377993062941850)
XLA Ops:
  0.0 1.0 %copy.15 = bf16[8,8,8,128]{3,2,1,0:T(8,128)(2,1)S(1)} copy(bf16[8,8,8,128]{3,1,2,0:T(8,128)(2,1)} %bitcast.60) | data formatting | bytes 262144
  1.0 0.9 %copy.16 = bf16[8,8,8,128]{3,2,1,0:T(8,128)(2,1)S(1)} copy(bf16[8,8,8,128]{3,1,2,0:T(8,128)(2,1)} %bitcast.61) | data formatting | bytes 262144
  2.1 0.8 broadcast_in_dim.107
  2.9 6.8 %all-to-all-start = ((bf16[16,64,256]{2,1,0:T(8,128)(2,1)}), bf16[16,64,256]{2,1,0:T(8,128)(2,1)S(1)}, u32[]{:S(2)}, u32[]{:S(2)}) async-start(bf16[16,64,256]{2,1,0:T(8,128)(2,1)} %bitcast.15), calls=%async_computation | async-start | bytes 1048576 | tf_op jit(solution)/shard_map/all_to_all | solution.py:247
  9.7 0.1 pad_dynamic-slice_fusion.1
  9.8 0.1 pad_dynamic-slice_fusion
  9.9 3.8 %convert_reduce_fusion = s32[2048]{0:T(1024)S(1)} fusion(s32[4608]{0:T(1024)S(1)} %pad_dynamic-slice_fusion.1, s32[2048]{0:T(1024)S(1)} %pad_dynamic-slice_fusion), kind=kLoop, calls=%fused_computation | loop fusion | flops 28309504 | bytes 34816 | tf_op jit(solution)/shard_map/reduce_sum | solution.py:207
  13.7 0.1 slice.21
  13.8 0.1 select_reduce_fusion.2
  13.9 0.1 convert_reduce_fusion.1
  14.0 0.1 select_reduce_fusion.5
  14.1 0.1 select_reduce_fusion.1
  14.2 0.1 convert_reduce_fusion.2
  14.3 0.7 slice.23
  15.0 1.1 %copy.18 = bf16[8,32,8,256]{3,2,0,1:T(8,128)(2,1)} copy(bf16[8,32,8,256]{3,2,1,0:T(8,128)(2,1)S(1)} %bitcast.57) | data formatting | bytes 2097152 | tf_op jit(solution)/shard_map/reshape | solution.py:255
  16.1 0.7 compare_select_fusion.9
  16.8 3.2 %all-to-all-done = bf16[16,64,256]{2,1,0:T(8,128)(2,1)S(1)} async-done(((bf16[16,64,256]{2,1,0:T(8,128)(2,1)}), bf16[16,64,256]{2,1,0:T(8,128)(2,1)S(1)}, u32[]{:S(2)}, u32[]{:S(2)}) %all-to-all-start) | async-done | bytes 524320 | tf_op jit(solution)/shard_map/all_to_all | solution.py:247
  20.0 3.5 %collective-permute-start.1 = (bf16[8,128,256]{2,1,0:T(8,128)(2,1)S(1)}, bf16[8,128,256]{2,1,0:T(8,128)(2,1)S(1)}, u32[]{:S(2)}, u32[]{:S(2)}) collective-permute-start(bf16[8,128,256]{2,1,0:T(8,128)(2,1)S(1)} %bitcast.50), channel_id=1, source_target_pairs={{0,32},{1,33},{2,34},{3,35},{4,36},{5,37},{6,38},{7,39},{8,40},{9,... | collective-permute-start | bytes 1572872 | tf_op jit(solution)/shard_map/ppermute | solution.py:227
  23.5 6.0 %all-to-all-start.1 = ((bf16[32,64,256]{2,1,0:T(8,128)(2,1)}), bf16[32,64,256]{2,1,0:T(8,128)(2,1)S(1)}, u32[]{:S(2)}, u32[]{:S(2)}) async-start(bf16[32,64,256]{2,1,0:T(8,128)(2,1)} %bitcast.48), calls=%async_computation.1 | async-start | bytes 2097152 | tf_op jit(solution)/shard_map/all_to_all | solution.py:257
  29.6 0.7 slice.22
  30.2 0.1 select_reduce_fusion.4
  30.3 4.9 %collective-permute-start.2 = (bf16[2,128,256]{2,1,0:T(8,128)(2,1)S(1)}, bf16[2,128,256]{2,1,0:T(8,128)(2,1)S(1)}, u32[]{:S(2)}, u32[]{:S(2)}) collective-permute-start(bf16[2,128,256]{2,1,0:T(8,128)(2,1)S(1)} %bitcast.62), channel_id=1, source_target_pairs={{0,64},{1,65},{2,66},{3,67},{4,68},{5,69},{6,70},{7,71},{8,72},{9,... | collective-permute-start | bytes 393224 | tf_op jit(solution)/shard_map/ppermute | solution.py:227
  35.2 0.7 compare_select_fusion.11
  37.4 2.5 %collective-permute-start = (bf16[8,128,256]{2,1,0:T(8,128)(2,1)S(1)}, bf16[8,128,256]{2,1,0:T(8,128)(2,1)S(1)}, u32[]{:S(2)}, u32[]{:S(2)}) collective-permute-start(bf16[8,128,256]{2,1,0:T(8,128)(2,1)S(1)} %bitcast.51), channel_id=1, source_target_pairs={{0,1},{1,0},{2,3},{3,2},{4,5},{5,4},{6,7},{7,6},{8,9},{9,8},{10,11... | collective-permute-start | bytes 1572872 | tf_op jit(solution)/shard_map/ppermute | solution.py:227
  39.9 2.0 %collective-permute-done.2.tail_m = bf16[2,128,256]{2,1,0:T(8,128)(2,1)S(1)} collective-permute-done((bf16[2,128,256]{2,1,0:T(8,128)(2,1)S(1)}, bf16[2,128,256]{2,1,0:T(8,128)(2,1)S(1)}, u32[]{:S(2)}, u32[]{:S(2)}) %collective-permute-start.2) | collective-permute-done | bytes 131104 | tf_op jit(solution)/shard_map/ppermute | solution.py:227
  41.9 3.1 %collective-permute-start.3 = (bf16[8,128,256]{2,1,0:T(8,128)(2,1)S(1)}, bf16[8,128,256]{2,1,0:T(8,128)(2,1)S(1)}, u32[]{:S(2)}, u32[]{:S(2)}) collective-permute-start(bf16[8,128,256]{2,1,0:T(8,128)(2,1)S(1)} %collective-permute-done.1.prev_m), channel_id=1, source_target_pairs={{0,1},{1,0},{2,3},{3,2},{4,5},{5,4},{6,7},{7,6},{8,9},{9,8},{10,11... | collective-permute-start | bytes 1572872 | tf_op jit(solution)/shard_map/ppermute | solution.py:227
  45.0 0.1 pad_add_fusion.3.info
  45.1 1.9 %collective-permute-start.4 = (bf16[2,128,256]{2,1,0:T(8,128)(2,1)S(1)}, bf16[2,128,256]{2,1,0:T(8,128)(2,1)S(1)}, u32[]{:S(2)}, u32[]{:S(2)}) collective-permute-start(bf16[2,128,256]{2,1,0:T(8,128)(2,1)S(1)} %collective-permute-done.2.tail_m), channel_id=1, source_target_pairs={{0,1},{1,0},{2,3},{3,2},{4,5},{5,4},{6,7},{7,6},{8,9},{9,8},{10,11... | collective-permute-start | bytes 393224 | tf_op jit(solution)/shard_map/ppermute | solution.py:227
  47.1 8.8 %shard_map.46 = (bf16[8,256,512]{2,1,0:T(8,128)(2,1)S(1)}, f32[8,144,512]{2,1,0:T(8,128)S(1)}, f32[8,1,512]{2,1,0:T(1,128)S(1)}) custom-call(s32[3,16]{1,0:T(4,128)S(1)} %pad_add_fusion.1.items, s32[2]{0:T(128)S(1)} %pad_add_fusion.3.info, bf16[2048,256]{1,0:T(8,128)(2,1)S(1)} %bitcast.49, s32[8,1,256]{2,1,0:T(1,128)S(1)} %add_maximum_fusion.starts_ref, ...), custom_call_target="tpu_custom_call" | custom-call | flops 1000000 | bytes 8388608 | tf_op jit(solution)/shard_map/pallas_call | solution.py:157
  56.0 8.7 %shard_map.47 = bf16[2048,256]{1,0:T(8,128)(2,1)S(1)} custom-call(s32[3,32]{1,0:T(4,128)S(1)} %pad_add_fusion.items, s32[2]{0:T(128)S(1)} %pad_add_fusion.2.info, s32[8,1,256]{2,1,0:T(1,128)S(1)} %bitcast.55, bf16[8,256,512]{2,1,0:T(8,128)(2,1)S(1)} %get-tuple-element.12.qt, f32[8,144,512]{2,1,0:T(8,128)S(1)} %get-tuple-element.13.acc_in, ...), custom_call_target="tpu_custom_call" | custom-call | flops 8000000000 | bytes 8388608 | tf_op jit(solution)/shard_map/pallas_call | solution.py:173
  64.7 24.3 %all_to_all.15 = bf16[32,64,256]{2,1,0:T(8,128)(2,1)S(1)} all-to-all(bf16[32,64,256]{2,1,0:T(8,128)(2,1)S(1)} %bitcast.53), channel_id=1, replica_groups=mesh['z'=16,'x'=4,'y'=4,'core'=2] {'x','y','core'}, dimensions={0} | all-to-all | bytes 2097152 | tf_op jit(solution)/shard_map/all_to_all | solution.py:262
  89.1 1.0 %copy.14 = bf16[32,8,8,256]{3,2,0,1:T(8,128)(2,1)} copy(bf16[32,8,8,256]{3,2,1,0:T(8,128)(2,1)S(1)} %bitcast.56) | data formatting | bytes 2097152 | tf_op jit(solution)/shard_map/reshape | solution.py:263
  (22 shorter events, 0.3 us)
Async XLA Ops:
  0.0 9.7 %copy-start.1 = (s32[32768]{0:T(1024)S(1)}, s32[32768]{0:T(1024)}, u32[]{:S(2)}) copy-start(s32[32768]{0:T(1024)} %param.7) | copy-start | bytes 393220
  0.0 15.0 %copy-start = (bf16[64,8192]{1,0:T(8,128)(2,1)S(1)}, bf16[64,8192]{1,0:T(8,128)(2,1)}, u32[]{:S(2)}) copy-start(bf16[64,8192]{1,0:T(8,128)(2,1)} %param.4) | copy-start | bytes 3145732
  2.9 17.1 %all-to-all-start = ((bf16[16,64,256]{2,1,0:T(8,128)(2,1)}), bf16[16,64,256]{2,1,0:T(8,128)(2,1)S(1)}, u32[]{:S(2)}, u32[]{:S(2)}) async-start(bf16[16,64,256]{2,1,0:T(8,128)(2,1)} %bitcast.15), calls=%async_computation | async-start | bytes 1048576 | tf_op jit(solution)/shard_map/all_to_all | solution.py:247
  20.0 22.0 %collective-permute-start.1 = (bf16[8,128,256]{2,1,0:T(8,128)(2,1)S(1)}, bf16[8,128,256]{2,1,0:T(8,128)(2,1)S(1)}, u32[]{:S(2)}, u32[]{:S(2)}) collective-permute-start(bf16[8,128,256]{2,1,0:T(8,128)(2,1)S(1)} %bitcast.50), channel_id=1, source_target_pairs={{0,32},{1,33},{2,34},{3,35},{4,36},{5,37},{6,38},{7,39},{8,40},{9,... | collective-permute-start | bytes 1572872 | tf_op jit(solution)/shard_map/ppermute | solution.py:227
  23.5 23.6 %all-to-all-start.1 = ((bf16[32,64,256]{2,1,0:T(8,128)(2,1)}), bf16[32,64,256]{2,1,0:T(8,128)(2,1)S(1)}, u32[]{:S(2)}, u32[]{:S(2)}) async-start(bf16[32,64,256]{2,1,0:T(8,128)(2,1)} %bitcast.48), calls=%async_computation.1 | async-start | bytes 2097152 | tf_op jit(solution)/shard_map/all_to_all | solution.py:257
  30.3 11.6 %collective-permute-start.2 = (bf16[2,128,256]{2,1,0:T(8,128)(2,1)S(1)}, bf16[2,128,256]{2,1,0:T(8,128)(2,1)S(1)}, u32[]{:S(2)}, u32[]{:S(2)}) collective-permute-start(bf16[2,128,256]{2,1,0:T(8,128)(2,1)S(1)} %bitcast.62), channel_id=1, source_target_pairs={{0,64},{1,65},{2,66},{3,67},{4,68},{5,69},{6,70},{7,71},{8,72},{9,... | collective-permute-start | bytes 393224 | tf_op jit(solution)/shard_map/ppermute | solution.py:227
  37.4 9.8 %collective-permute-start = (bf16[8,128,256]{2,1,0:T(8,128)(2,1)S(1)}, bf16[8,128,256]{2,1,0:T(8,128)(2,1)S(1)}, u32[]{:S(2)}, u32[]{:S(2)}) collective-permute-start(bf16[8,128,256]{2,1,0:T(8,128)(2,1)S(1)} %bitcast.51), channel_id=1, source_target_pairs={{0,1},{1,0},{2,3},{3,2},{4,5},{5,4},{6,7},{7,6},{8,9},{9,8},{10,11... | collective-permute-start | bytes 1572872 | tf_op jit(solution)/shard_map/ppermute | solution.py:227
  41.9 14.0 %collective-permute-start.3 = (bf16[8,128,256]{2,1,0:T(8,128)(2,1)S(1)}, bf16[8,128,256]{2,1,0:T(8,128)(2,1)S(1)}, u32[]{:S(2)}, u32[]{:S(2)}) collective-permute-start(bf16[8,128,256]{2,1,0:T(8,128)(2,1)S(1)} %collective-permute-done.1.prev_m), channel_id=1, source_target_pairs={{0,1},{1,0},{2,3},{3,2},{4,5},{5,4},{6,7},{7,6},{8,9},{9,8},{10,11... | collective-permute-start | bytes 1572872 | tf_op jit(solution)/shard_map/ppermute | solution.py:227
  45.1 10.8 %collective-permute-start.4 = (bf16[2,128,256]{2,1,0:T(8,128)(2,1)S(1)}, bf16[2,128,256]{2,1,0:T(8,128)(2,1)S(1)}, u32[]{:S(2)}, u32[]{:S(2)}) collective-permute-start(bf16[2,128,256]{2,1,0:T(8,128)(2,1)S(1)} %collective-permute-done.2.tail_m), channel_id=1, source_target_pairs={{0,1},{1,0},{2,3},{3,2},{4,5},{5,4},{6,7},{7,6},{8,9},{9,8},{10,11... | collective-permute-start | bytes 393224 | tf_op jit(solution)/shard_map/ppermute | solution.py:227

commit v3 on v2

--- a/solution.py
+++ b/solution.py
@@ -26,7 +26,7 @@
 VMEM = pltpu.VMEM
 
 
-def work(items, info, starts_ref, causal, ks, vt, qt, spot, acc, peak, sa, sb):
+def work(items, info, starts_ref, ks, vt, qt, spot, acc, peak, sa, sb):
     def scored(number, buffer):
         tile, first = items[0, number], items[1, number]
         keys = ks[pl.ds(first, SPAN)].reshape(SPAN * GRAN, 2 * HD)
@@ -37,8 +37,8 @@
         for k in range(SPAN):
             rows = slice(k * GRAN, (k + 1) * GRAN)
             seen = place >= jnp.concatenate([low - k * GRAN] * HEADS, axis=1)
-            if causal and k == SPAN - 1:
-                own = (tile - first) * GRAN + lax.broadcasted_iota(jnp.int32, (1, GRAN), 1)
+            if k == SPAN - 1:
+                own = (BACK + tile - first) * GRAN + lax.broadcasted_iota(jnp.int32, (1, GRAN), 1)
                 seen = seen & (place <= jnp.concatenate([own] * HEADS, axis=1))
             piece = jnp.where(seen, raw[rows], HIDDEN)
             buffer[rows] = piece
@@ -97,8 +97,13 @@
         vt[:HD, (PAD + g) * GRAN:(PAD + g + 1) * GRAN] = stage[g].T
 
 
-def own_kernel(items, info, q_ref, starts_ref, own_m, own_o, qt, acc, peak, ks, vt, stage, spot, sa, sb, sems):
-    copies = fill(info, ((0, OWN, (own_m, own_o)),), ks, vt, stage, spot, sems)
+def kernel(
+    items, info, q_ref, starts_ref, own_m, own_o, prev_m, prev_o, tail_m, tail_o,
+    o_ref, qt, acc, peak, ks, vt, stage, spot, sa, sb, sems,
+):
+    tail = BACK - OWN
+    groups = (BACK, OWN, (own_m, own_o)), (tail, OWN, (prev_m, prev_o)), (0, tail, (tail_m, tail_o))
+    copies = fill(info, groups, ks, vt, stage, spot, sems)
     acc[...] = jnp.zeros_like(acc)
     peak[...] = jnp.full_like(peak, HIDDEN)
     for tile in range(OWN):
@@ -110,22 +115,8 @@
             qt[tile, HD:, cols] = (query - coarse.astype(jnp.float32)).astype(jnp.bfloat16)
     for copy in copies:
         copy.wait()
-    turn(OWN, vt, stage)
-    work(items, info, starts_ref, True, ks, vt, qt, spot, acc, peak, sa, sb)
-
-
-def back_kernel(
-    items, info, starts_ref, qt, acc_in, peak_in, prev_m, prev_o, tail_m, tail_o,
-    o_ref, acc, peak, ks, vt, stage, spot, sa, sb, sems,
-):
-    tail = BACK - OWN
-    copies = fill(info, ((tail, OWN, (prev_m, prev_o)), (0, tail, (tail_m, tail_o))), ks, vt, stage, spot, sems)
-    acc[...] = acc_in[...]
-    peak[...] = peak_in[...]
-    for copy in copies:
-        copy.wait()
-    turn(BACK, vt, stage)
-    work(items, info, starts_ref, False, ks, vt, qt, spot, acc, peak, sa, sb)
+    turn(BACK + OWN, vt, stage)
+    work(items, info, starts_ref, ks, vt, qt, spot, acc, peak, sa, sb)
     for tile in range(OWN):
         for head in range(HEADS):
             cols = slice(head * GRAN, (head + 1) * GRAN)
@@ -134,55 +125,54 @@
             )
 
 
-def scratch(granules, copies):
-    return [
-        VMEM((PAD + granules, GRAN, 2 * HD), jnp.bfloat16),
-        VMEM((HD + ONES, (PAD + granules) * GRAN), jnp.bfloat16),
-        VMEM((granules, GRAN, HD), jnp.bfloat16),
-        VMEM((GRAN, HD), jnp.int32),
-        VMEM((SPAN * GRAN, COLS), jnp.float32),
-        VMEM((SPAN * GRAN, COLS), jnp.float32),
-        pltpu.SemaphoreType.DMA((copies,)),
-    ]
-
-
-STATE = ((OWN, HD + ONES, COLS), jnp.float32), ((OWN, 1, COLS), jnp.float32)
 LIMIT = pltpu.CompilerParams(vmem_limit_bytes=40 * 1024 * 1024)
 INSIDE = pl.BlockSpec(memory_space=VMEM)
 ANYWHERE = pl.BlockSpec(memory_space=pl.ANY)
 
 
-def attend_own(items, info, queries, starts, pair):
-    shapes = (((OWN, 2 * HD, COLS), jnp.bfloat16),) + STATE
+def attend(items, info, queries, starts, pieces):
+    window = BACK + OWN
     return pl.pallas_call(
-        own_kernel,
+        kernel,
         grid_spec=pltpu.PrefetchScalarGridSpec(
             num_scalar_prefetch=2,
             grid=(),
-            in_specs=[INSIDE, INSIDE, ANYWHERE, ANYWHERE],
-            out_specs=[INSIDE] * 3,
-            scratch_shapes=scratch(OWN, 6),
-        ),
-        out_shape=[jax.ShapeDtypeStruct(*s) for s in shapes],
-        compiler_params=LIMIT,
-        cost_estimate=pl.CostEstimate(flops=10**6, bytes_accessed=8 << 20, transcendentals=0),
-    )(items, info, queries, starts, *pair)
-
-
-def attend_back(items, info, starts, state, pieces):
-    return pl.pallas_call(
-        back_kernel,
-        grid_spec=pltpu.PrefetchScalarGridSpec(
-            num_scalar_prefetch=2,
-            grid=(),
-            in_specs=[INSIDE] * 4 + [ANYWHERE] * 4,
+            in_specs=[INSIDE] * 2 + [ANYWHERE] * 6,
             out_specs=INSIDE,
-            scratch_shapes=[VMEM(*s) for s in STATE] + scratch(BACK, 12),
+            scratch_shapes=[
+                VMEM((OWN, 2 * HD, COLS), jnp.bfloat16),
+                VMEM((OWN, HD + ONES, COLS), jnp.float32),
+                VMEM((OWN, 1, COLS), jnp.float32),
+                VMEM((PAD + window, GRAN, 2 * HD), jnp.bfloat16),
+                VMEM((HD + ONES, (PAD + window) * GRAN), jnp.bfloat16),
+                VMEM((window, GRAN, HD), jnp.bfloat16),
+                VMEM((GRAN, HD), jnp.int32),
+                VMEM((SPAN * GRAN, COLS), jnp.float32),
+                VMEM((SPAN * GRAN, COLS), jnp.float32),
+                pltpu.SemaphoreType.DMA((18,)),
+            ],
         ),
         out_shape=jax.ShapeDtypeStruct((OWN * GRAN, HEADS * HD), jnp.bfloat16),
         compiler_params=LIMIT,
-        cost_estimate=pl.CostEstimate(flops=8 * 10**9, bytes_accessed=8 << 20, transcendentals=0),
-    )(items, info, starts, *state, *pieces)
+        cost_estimate=pl.CostEstimate(flops=10**10, bytes_accessed=8 << 20, transcendentals=0),
+    )(items, info, queries, starts, *pieces)
+
+
+def pack_kernel(k_ref, v_ref, o_ref):
+    copies = o_ref.shape[0] * HD // k_ref.shape[1]
+    for place in range(o_ref.shape[0]):
+        cols = slice(place // copies * HD, (place // copies + 1) * HD)
+        o_ref[place, :, :HD] = k_ref[:, cols]
+        o_ref[place, :, HD:] = v_ref[:, cols]
+
+
+def pack(keys, values, chips):
+    return pl.pallas_call(
+        pack_kernel,
+        in_specs=[INSIDE] * 2,
+        out_specs=INSIDE,
+        out_shape=jax.ShapeDtypeStruct((chips, keys.shape[0], 2 * HD), jnp.bfloat16),
+    )(keys, values)
 
 
 def agenda(counts, tops, room, core):
@@ -207,10 +197,8 @@
     starts = jnp.sum(window[None, :] < ids[:, None], axis=1, dtype=jnp.int32)
     lows = starts[::GRAN] // GRAN
     tiles = jnp.arange(OWN, dtype=jnp.int32)
-    mine = agenda((tiles - jnp.maximum(lows - BACK, 0)) // SPAN + 1, tiles, 16, core)
-    older = agenda((jnp.maximum(BACK - lows, 0) + SPAN - 1) // SPAN, jnp.full((OWN,), BACK - 1, jnp.int32), 32, core)
-    starts = starts.reshape(OWN, 1, GRAN)
-    return mine, older, jnp.maximum(starts - BACK * GRAN, 0), starts
+    items, info = agenda((BACK + tiles - lows) // SPAN + 1, BACK + tiles, 32, core)
+    return items, info, starts.reshape(OWN, 1, GRAN)
 
 
 def moved(value, sizes, there):
@@ -232,7 +220,6 @@
     chips = xs * ys
     teams = chips * cores
     tokens = queries.shape[0]
-    key_heads = keys.shape[1] // HD
     plane = OWN * GRAN
 
     def swap(value):
@@ -241,10 +228,7 @@
     def later(value, planes):
         return moved(value, sizes, lambda z, x, y, core: (z + planes, x, y, core) if z + planes < zs else None)
 
-    both = jnp.stack([keys.reshape(tokens, key_heads, HD), values.reshape(tokens, key_heads, HD)], axis=2)
-    both = jnp.transpose(both.reshape(tokens, key_heads, 2 * HD), (1, 0, 2))
-    both = jnp.repeat(both, chips // key_heads, axis=0)
-    own_m = lax.all_to_all(both, ("x", "y"), 0, 0, tiled=True).reshape(OWN, HALF, 2 * HD)
+    own_m = lax.all_to_all(pack(keys, values, chips), ("x", "y"), 0, 0, tiled=True).reshape(OWN, HALF, 2 * HD)
     prev_m = later(own_m, 1)
     tail_m = later(own_m[2 * OWN - BACK:], 2)
     prev_m, tail_m = lax.optimization_barrier((prev_m, tail_m))
@@ -256,9 +240,8 @@
     wide, _ = lax.optimization_barrier((wide, own_m))
     local = lax.all_to_all(wide, ("x", "y", "core"), 0, 0, tiled=True).reshape(plane, HEADS * HD)
 
-    mine, older, near, far = plans(doc_ids, lax.axis_index("z") * plane, lax.axis_index("core"))
-    state = attend_own(*mine, local, near, (own_m, own_o))
-    out = attend_back(*older, far, state, (prev_m, prev_o, tail_m, tail_o))
+    items, info, starts = plans(doc_ids, lax.axis_index("z") * plane, lax.axis_index("core"))
+    out = attend(items, info, local, starts, (own_m, own_o, prev_m, prev_o, tail_m, tail_o))
     back = lax.all_to_all(out.reshape(teams, tokens, HEADS * HD), ("x", "y", "core"), 0, 0, tiled=True)
     return jnp.transpose(back, (1, 0, 2)).reshape(tokens, teams * HEADS * HD)
 

time: 90.6 us -> 87.5 us (0.966)
  waiting for transfers between devices: 5.22 us -> 8.92 us
  local copies, waits for them, and re-layouts: 6.58 us -> 3.08 us
  other arithmetic: 6.07 us -> 4.93 us
  Pallas kernels: 17.5 us -> 16.4 us
    unnamed x6 -> x4, local copies, waits for them, and re-layouts: 1.95 us -> 0.01 us
    ppermute x5, waiting for transfers between devices: 2.03 us -> 3.96 us  [moved(): return lax.ppermute(value, AXES, pairs)]
    all_to_all x1, waiting for transfers between devices: 3.18 us -> 4.96 us  [body(): lax.all_to_all(pack(keys, values, chips), ('x', 'y'), 0, 0, tiled=True)]
    pallas_call x2, Pallas kernels: 17.5 us -> 16.4 us  [the longest x1 14.5 us: attend(): pl.pallas_call(kernel, grid_spec=pltpu.PrefetchScalarGridSpec(num_scalar_...]
  transfers between devices with their start and end apart: 7 -> 7, of which waited for: 2 -> 3; matrix products, arithmetic and copies ran while one was open for 10% -> 8% of each run, Pallas kernels for 10% -> 0%
where the time goes in v3:
time: 87.5 us; the launch traced here: 87 us
  starting transfers between devices  28.8 us (33%)
  blocking collectives  23.9 us (27%)
  Pallas kernels  16.4 us (19%)
  waiting for transfers between devices  8.92 us (10%)
  other arithmetic  4.93 us (6%)
  local copies, waits for them, and re-layouts  3.08 us (4%)
    all_to_all x1, blocking collectives, body(): lax.all_to_all(out.reshape(teams, tokens, HEADS * HD), ('x', 'y', 'core')...  23.9 us
    ppermute x5, starting transfers between devices, moved(): return lax.ppermute(value, AXES, pairs)  16.1 us
    pallas_call x1, Pallas kernels, attend(): pl.pallas_call(kernel, grid_spec=pltpu.PrefetchScalarGridSpec(num_scalar_...  14.5 us
    all_to_all x1, starting transfers between devices, body(): lax.all_to_all(pack(keys, values, chips), ('x', 'y'), 0, 0, tiled=True)  6.75 us
    all_to_all x1, starting transfers between devices, body(): lax.all_to_all(wide, ('x', 'y', 'core'), 0, 0, tiled=True)  6.02 us
    all_to_all x1, waiting for transfers between devices, body(): lax.all_to_all(pack(keys, values, chips), ('x', 'y'), 0, 0, tiled=True)  4.96 us
    ppermute x5, waiting for transfers between devices, moved(): return lax.ppermute(value, AXES, pairs)  3.96 us
    reduce_sum x1, other arithmetic, plans(): starts = jnp.sum(window[None, :] < ids[:, None], axis=1, dtype=jnp.int32)  3.81 us
  transfers between devices with their start and end apart: 7, of which 3 were waited for; matrix products, arithmetic and copies ran while one was open for 8% of the time, Pallas kernels for 0%

profile of v3, /device:TPU:129, one launch (start us, length us, event | category | flops | bytes accessed | tf_op | source)
XLA Modules:
  0.0 87.0 jit_solution(14421769430986988682)
XLA Ops:
  0.0 0.0 copy-start.1
  0.0 1.9 %shard_map.46 = bf16[16,64,256]{2,1,0:T(8,128)(2,1)} custom-call(bf16[64,1024]{1,0:T(8,128)(2,1)} %k_ref.1, bf16[64,1024]{1,0:T(8,128)(2,1)} %v_ref.1), custom_call_target="tpu_custom_call" | custom-call | tf_op jit(solution)/shard_map/pallas_call | solution.py:170
  1.9 6.8 %all-to-all-start = ((bf16[16,64,256]{2,1,0:T(8,128)(2,1)}), bf16[16,64,256]{2,1,0:T(8,128)(2,1)S(1)}, u32[]{:S(2)}, u32[]{:S(2)}) async-start(bf16[16,64,256]{2,1,0:T(8,128)(2,1)} %shard_map.46), calls=%async_computation | async-start | bytes 1048576 | tf_op jit(solution)/shard_map/all_to_all | solution.py:231
  8.7 0.0 copy-done.1
  8.7 0.1 pad_dynamic-slice_fusion.1
  8.8 0.1 pad_dynamic-slice_fusion
  8.9 3.8 %convert_reduce_fusion = s32[2048]{0:T(1024)S(1)} fusion(s32[4608]{0:T(1024)S(1)} %pad_dynamic-slice_fusion.1, s32[2048]{0:T(1024)S(1)} %pad_dynamic-slice_fusion), kind=kLoop, calls=%fused_computation | loop fusion | flops 28309504 | bytes 34816 | tf_op jit(solution)/shard_map/reduce_sum | solution.py:197
  12.7 0.1 slice.17
  12.8 0.0 copy-done
  12.8 1.1 %copy.12 = bf16[8,32,8,256]{3,2,0,1:T(8,128)(2,1)} copy(bf16[8,32,8,256]{3,2,1,0:T(8,128)(2,1)S(1)} %bitcast.33) | data formatting | bytes 2097152 | tf_op jit(solution)/shard_map/reshape | solution.py:239
  13.9 0.1 select_reduce_fusion.2
  14.0 5.0 %all-to-all-done = bf16[16,64,256]{2,1,0:T(8,128)(2,1)S(1)} async-done(((bf16[16,64,256]{2,1,0:T(8,128)(2,1)}), bf16[16,64,256]{2,1,0:T(8,128)(2,1)S(1)}, u32[]{:S(2)}, u32[]{:S(2)}) %all-to-all-start) | async-done | bytes 524320 | tf_op jit(solution)/shard_map/all_to_all | solution.py:231
  19.0 3.5 %collective-permute-start.1 = (bf16[8,128,256]{2,1,0:T(8,128)(2,1)S(1)}, bf16[8,128,256]{2,1,0:T(8,128)(2,1)S(1)}, u32[]{:S(2)}, u32[]{:S(2)}) collective-permute-start(bf16[8,128,256]{2,1,0:T(8,128)(2,1)S(1)} %bitcast.28), channel_id=1, source_target_pairs={{0,32},{1,33},{2,34},{3,35},{4,36},{5,37},{6,38},{7,39},{8,40},{9,... | collective-permute-start | bytes 1572872 | tf_op jit(solution)/shard_map/ppermute | solution.py:215
  22.5 6.0 %all-to-all-start.1 = ((bf16[32,64,256]{2,1,0:T(8,128)(2,1)}), bf16[32,64,256]{2,1,0:T(8,128)(2,1)S(1)}, u32[]{:S(2)}, u32[]{:S(2)}) async-start(bf16[32,64,256]{2,1,0:T(8,128)(2,1)} %bitcast.25), calls=%async_computation.1 | async-start | bytes 2097152 | tf_op jit(solution)/shard_map/all_to_all | solution.py:241
  28.6 0.1 convert_reduce_fusion.1
  28.7 4.9 %collective-permute-start.2 = (bf16[2,128,256]{2,1,0:T(8,128)(2,1)S(1)}, bf16[2,128,256]{2,1,0:T(8,128)(2,1)S(1)}, u32[]{:S(2)}, u32[]{:S(2)}) collective-permute-start(bf16[2,128,256]{2,1,0:T(8,128)(2,1)S(1)} %bitcast.34), channel_id=1, source_target_pairs={{0,64},{1,65},{2,66},{3,67},{4,68},{5,69},{6,70},{7,71},{8,72},{9,... | collective-permute-start | bytes 393224 | tf_op jit(solution)/shard_map/ppermute | solution.py:215
  33.6 0.7 slice.18
  35.0 2.5 %collective-permute-start = (bf16[8,128,256]{2,1,0:T(8,128)(2,1)S(1)}, bf16[8,128,256]{2,1,0:T(8,128)(2,1)S(1)}, u32[]{:S(2)}, u32[]{:S(2)}) collective-permute-start(bf16[8,128,256]{2,1,0:T(8,128)(2,1)S(1)} %bitcast.29), channel_id=1, source_target_pairs={{0,1},{1,0},{2,3},{3,2},{4,5},{5,4},{6,7},{7,6},{8,9},{9,8},{10,11... | collective-permute-start | bytes 1572872 | tf_op jit(solution)/shard_map/ppermute | solution.py:215
  37.5 2.7 %collective-permute-done.2.tail_m = bf16[2,128,256]{2,1,0:T(8,128)(2,1)S(1)} collective-permute-done((bf16[2,128,256]{2,1,0:T(8,128)(2,1)S(1)}, bf16[2,128,256]{2,1,0:T(8,128)(2,1)S(1)}, u32[]{:S(2)}, u32[]{:S(2)}) %collective-permute-start.2) | collective-permute-done | bytes 131104 | tf_op jit(solution)/shard_map/ppermute | solution.py:215
  40.3 0.0 collective-permute-done.1.prev_m
  40.3 3.2 %collective-permute-start.3 = (bf16[8,128,256]{2,1,0:T(8,128)(2,1)S(1)}, bf16[8,128,256]{2,1,0:T(8,128)(2,1)S(1)}, u32[]{:S(2)}, u32[]{:S(2)}) collective-permute-start(bf16[8,128,256]{2,1,0:T(8,128)(2,1)S(1)} %collective-permute-done.1.prev_m), channel_id=1, source_target_pairs={{0,1},{1,0},{2,3},{3,2},{4,5},{5,4},{6,7},{7,6},{8,9},{9,8},{10,11... | collective-permute-start | bytes 1572872 | tf_op jit(solution)/shard_map/ppermute | solution.py:215
  43.5 0.1 select_reduce_fusion.1
  43.5 0.7 compare_select_fusion.6
  44.2 1.9 %collective-permute-start.4 = (bf16[2,128,256]{2,1,0:T(8,128)(2,1)S(1)}, bf16[2,128,256]{2,1,0:T(8,128)(2,1)S(1)}, u32[]{:S(2)}, u32[]{:S(2)}) collective-permute-start(bf16[2,128,256]{2,1,0:T(8,128)(2,1)S(1)} %collective-permute-done.2.tail_m), channel_id=1, source_target_pairs={{0,1},{1,0},{2,3},{3,2},{4,5},{5,4},{6,7},{7,6},{8,9},{9,8},{10,11... | collective-permute-start | bytes 393224 | tf_op jit(solution)/shard_map/ppermute | solution.py:215
  46.2 0.1 pad_add_fusion.1.info
  46.3 0.0 collective-permute-done.own_o
  46.3 1.2 %collective-permute-done.4.tail_o = bf16[2,128,256]{2,1,0:T(8,128)(2,1)S(1)} collective-permute-done((bf16[2,128,256]{2,1,0:T(8,128)(2,1)S(1)}, bf16[2,128,256]{2,1,0:T(8,128)(2,1)S(1)}, u32[]{:S(2)}, u32[]{:S(2)}) %collective-permute-start.4) | collective-permute-done | bytes 131104 | tf_op jit(solution)/shard_map/ppermute | solution.py:215
  47.5 0.0 all-to-all-done.1
  47.5 0.0 collective-permute-done.3.prev_o
  47.5 14.5 %shard_map.47 = bf16[2048,256]{1,0:T(8,128)(2,1)S(1)} custom-call(s32[3,32]{1,0:T(4,128)S(1)} %pad_add_fusion.items, s32[2]{0:T(128)S(1)} %pad_add_fusion.1.info, bf16[2048,256]{1,0:T(8,128)(2,1)S(1)} %bitcast.26, s32[8,1,256]{2,1,0:T(1,128)S(1)} %bitcast.31, bf16[8,128,256]{2,1,0:T(8,128)(2,1)S(1)} %bitcast.30, ...), custom_call_target="tpu_custom_call" | custom-call | flops 10000000000 | bytes 8388608 | tf_op jit(solution)/shard_map/pallas_call | solution.py:135
  62.0 23.9 %all_to_all.15 = bf16[32,64,256]{2,1,0:T(8,128)(2,1)S(1)} all-to-all(bf16[32,64,256]{2,1,0:T(8,128)(2,1)S(1)} %bitcast.27), channel_id=1, replica_groups=mesh['z'=16,'x'=4,'y'=4,'core'=2] {'x','y','core'}, dimensions={0} | all-to-all | bytes 2097152 | tf_op jit(solution)/shard_map/all_to_all | solution.py:245
  85.9 1.0 %copy.10 = bf16[32,8,8,256]{3,2,0,1:T(8,128)(2,1)} copy(bf16[32,8,8,256]{3,2,1,0:T(8,128)(2,1)S(1)} %bitcast.32) | data formatting | bytes 2097152 | tf_op jit(solution)/shard_map/reshape | solution.py:246
  (7 shorter events, 0.1 us)
Async XLA Ops:
  0.0 8.7 %copy-start.1 = (s32[32768]{0:T(1024)S(1)}, s32[32768]{0:T(1024)}, u32[]{:S(2)}) copy-start(s32[32768]{0:T(1024)} %param.7) | copy-start | bytes 393220
  0.0 12.8 %copy-start = (bf16[64,8192]{1,0:T(8,128)(2,1)S(1)}, bf16[64,8192]{1,0:T(8,128)(2,1)}, u32[]{:S(2)}) copy-start(bf16[64,8192]{1,0:T(8,128)(2,1)} %param.4) | copy-start | bytes 3145732
  1.9 17.1 %all-to-all-start = ((bf16[16,64,256]{2,1,0:T(8,128)(2,1)}), bf16[16,64,256]{2,1,0:T(8,128)(2,1)S(1)}, u32[]{:S(2)}, u32[]{:S(2)}) async-start(bf16[16,64,256]{2,1,0:T(8,128)(2,1)} %shard_map.46), calls=%async_computation | async-start | bytes 1048576 | tf_op jit(solution)/shard_map/all_to_all | solution.py:231
  19.0 21.3 %collective-permute-start.1 = (bf16[8,128,256]{2,1,0:T(8,128)(2,1)S(1)}, bf16[8,128,256]{2,1,0:T(8,128)(2,1)S(1)}, u32[]{:S(2)}, u32[]{:S(2)}) collective-permute-start(bf16[8,128,256]{2,1,0:T(8,128)(2,1)S(1)} %bitcast.28), channel_id=1, source_target_pairs={{0,32},{1,33},{2,34},{3,35},{4,36},{5,37},{6,38},{7,39},{8,40},{9,... | collective-permute-start | bytes 1572872 | tf_op jit(solution)/shard_map/ppermute | solution.py:215
  22.5 25.0 %all-to-all-start.1 = ((bf16[32,64,256]{2,1,0:T(8,128)(2,1)}), bf16[32,64,256]{2,1,0:T(8,128)(2,1)S(1)}, u32[]{:S(2)}, u32[]{:S(2)}) async-start(bf16[32,64,256]{2,1,0:T(8,128)(2,1)} %bitcast.25), calls=%async_computation.1 | async-start | bytes 2097152 | tf_op jit(solution)/shard_map/all_to_all | solution.py:241
  28.7 11.6 %collective-permute-start.2 = (bf16[2,128,256]{2,1,0:T(8,128)(2,1)S(1)}, bf16[2,128,256]{2,1,0:T(8,128)(2,1)S(1)}, u32[]{:S(2)}, u32[]{:S(2)}) collective-permute-start(bf16[2,128,256]{2,1,0:T(8,128)(2,1)S(1)} %bitcast.34), channel_id=1, source_target_pairs={{0,64},{1,65},{2,66},{3,67},{4,68},{5,69},{6,70},{7,71},{8,72},{9,... | collective-permute-start | bytes 393224 | tf_op jit(solution)/shard_map/ppermute | solution.py:215
  35.0 11.3 %collective-permute-start = (bf16[8,128,256]{2,1,0:T(8,128)(2,1)S(1)}, bf16[8,128,256]{2,1,0:T(8,128)(2,1)S(1)}, u32[]{:S(2)}, u32[]{:S(2)}) collective-permute-start(bf16[8,128,256]{2,1,0:T(8,128)(2,1)S(1)} %bitcast.29), channel_id=1, source_target_pairs={{0,1},{1,0},{2,3},{3,2},{4,5},{5,4},{6,7},{7,6},{8,9},{9,8},{10,11... | collective-permute-start | bytes 1572872 | tf_op jit(solution)/shard_map/ppermute | solution.py:215
  40.3 7.2 %collective-permute-start.3 = (bf16[8,128,256]{2,1,0:T(8,128)(2,1)S(1)}, bf16[8,128,256]{2,1,0:T(8,128)(2,1)S(1)}, u32[]{:S(2)}, u32[]{:S(2)}) collective-permute-start(bf16[8,128,256]{2,1,0:T(8,128)(2,1)S(1)} %collective-permute-done.1.prev_m), channel_id=1, source_target_pairs={{0,1},{1,0},{2,3},{3,2},{4,5},{5,4},{6,7},{7,6},{8,9},{9,8},{10,11... | collective-permute-start | bytes 1572872 | tf_op jit(solution)/shard_map/ppermute | solution.py:215
  44.2 3.2 %collective-permute-start.4 = (bf16[2,128,256]{2,1,0:T(8,128)(2,1)S(1)}, bf16[2,128,256]{2,1,0:T(8,128)(2,1)S(1)}, u32[]{:S(2)}, u32[]{:S(2)}) collective-permute-start(bf16[2,128,256]{2,1,0:T(8,128)(2,1)S(1)} %collective-permute-done.2.tail_m), channel_id=1, source_target_pairs={{0,1},{1,0},{2,3},{3,2},{4,5},{5,4},{6,7},{7,6},{8,9},{9,8},{10,11... | collective-permute-start | bytes 393224 | tf_op jit(solution)/shard_map/ppermute | solution.py:215

commit v4 on v3

--- a/solution.py
+++ b/solution.py
@@ -229,12 +229,14 @@
         return moved(value, sizes, lambda z, x, y, core: (z + planes, x, y, core) if z + planes < zs else None)
 
     own_m = lax.all_to_all(pack(keys, values, chips), ("x", "y"), 0, 0, tiled=True).reshape(OWN, HALF, 2 * HD)
-    prev_m = later(own_m, 1)
-    tail_m = later(own_m[2 * OWN - BACK:], 2)
-    prev_m, tail_m = lax.optimization_barrier((prev_m, tail_m))
+    end = own_m[2 * OWN - BACK:]
+    tail_m = later(end, 2)
+    whole, _ = lax.optimization_barrier((own_m, end))
+    prev_m = later(whole, 1)
     own_o = swap(own_m)
-    prev_o = swap(prev_m)
     tail_o = swap(tail_m)
+    ready, _ = lax.optimization_barrier((prev_m, tail_o))
+    prev_o = swap(ready)
 
     wide = jnp.transpose(queries.reshape(tokens, teams, HEADS * HD), (1, 0, 2))
     wide, _ = lax.optimization_barrier((wide, own_m))

time: 87.5 us -> 89.2 us (1.019)
  the two profiles are of different devices: /device:TPU:129 before, /device:TPU:33 now
where the time goes in v4:
time: 89.2 us; the launch traced here: 88.7 us
  starting transfers between devices  29.3 us (33%)
  blocking collectives  20.6 us (23%)
  Pallas kernels  16.9 us (19%)
  waiting for transfers between devices  12.9 us (14%)
  other arithmetic  4.93 us (6%)
  local copies, waits for them, and re-layouts  3.08 us (3%)
    all_to_all x1, blocking collectives, body(): lax.all_to_all(out.reshape(teams, tokens, HEADS * HD), ('x', 'y', 'core')...  20.6 us
    ppermute x5, starting transfers between devices, moved(): return lax.ppermute(value, AXES, pairs)  16.2 us
    pallas_call x1, Pallas kernels, attend(): pl.pallas_call(kernel, grid_spec=pltpu.PrefetchScalarGridSpec(num_scalar_...  15 us
    all_to_all x1, waiting for transfers between devices, body(): lax.all_to_all(wide, ('x', 'y', 'core'), 0, 0, tiled=True)  7.97 us
    all_to_all x1, starting transfers between devices, body(): lax.all_to_all(pack(keys, values, chips), ('x', 'y'), 0, 0, tiled=True)  6.75 us
    all_to_all x1, starting transfers between devices, body(): lax.all_to_all(wide, ('x', 'y', 'core'), 0, 0, tiled=True)  6.3 us
    all_to_all x1, waiting for transfers between devices, body(): lax.all_to_all(pack(keys, values, chips), ('x', 'y'), 0, 0, tiled=True)  4.97 us
    reduce_sum x1, other arithmetic, plans(): starts = jnp.sum(window[None, :] < ids[:, None], axis=1, dtype=jnp.int32)  3.81 us
  transfers between devices with their start and end apart: 7, of which 2 were waited for; matrix products, arithmetic and copies ran while one was open for 8% of the time, Pallas kernels for 0%

profile of v4, /device:TPU:33, one launch (start us, length us, event | category | flops | bytes accessed | tf_op | source)
XLA Modules:
  0.0 88.7 jit_solution(10474286886318145565)
XLA Ops:
  0.0 0.0 copy-start.1
  0.0 1.9 %shard_map.46 = bf16[16,64,256]{2,1,0:T(8,128)(2,1)} custom-call(bf16[64,1024]{1,0:T(8,128)(2,1)} %k_ref.1, bf16[64,1024]{1,0:T(8,128)(2,1)} %v_ref.1), custom_call_target="tpu_custom_call" | custom-call | tf_op jit(solution)/shard_map/pallas_call | solution.py:170
  1.9 6.8 %all-to-all-start = ((bf16[16,64,256]{2,1,0:T(8,128)(2,1)}), bf16[16,64,256]{2,1,0:T(8,128)(2,1)S(1)}, u32[]{:S(2)}, u32[]{:S(2)}) async-start(bf16[16,64,256]{2,1,0:T(8,128)(2,1)} %shard_map.46), calls=%async_computation | async-start | bytes 1048576 | tf_op jit(solution)/shard_map/all_to_all | solution.py:231
  8.7 0.0 copy-done.1
  8.7 0.1 pad_dynamic-slice_fusion.1
  8.8 0.1 pad_dynamic-slice_fusion
  8.9 3.8 %convert_reduce_fusion = s32[2048]{0:T(1024)S(1)} fusion(s32[4608]{0:T(1024)S(1)} %pad_dynamic-slice_fusion.1, s32[2048]{0:T(1024)S(1)} %pad_dynamic-slice_fusion), kind=kLoop, calls=%fused_computation | loop fusion | flops 28309504 | bytes 34816 | tf_op jit(solution)/shard_map/reduce_sum | solution.py:197
  12.7 0.1 slice.17
  12.8 0.0 copy-done
  12.8 1.1 %copy.12 = bf16[8,32,8,256]{3,2,0,1:T(8,128)(2,1)} copy(bf16[8,32,8,256]{3,2,1,0:T(8,128)(2,1)S(1)} %bitcast.33) | data formatting | bytes 2097152 | tf_op jit(solution)/shard_map/reshape | solution.py:241
  13.9 0.1 select_reduce_fusion.2
  14.0 5.0 %all-to-all-done = bf16[16,64,256]{2,1,0:T(8,128)(2,1)S(1)} async-done(((bf16[16,64,256]{2,1,0:T(8,128)(2,1)}), bf16[16,64,256]{2,1,0:T(8,128)(2,1)S(1)}, u32[]{:S(2)}, u32[]{:S(2)}) %all-to-all-start) | async-done | bytes 524320 | tf_op jit(solution)/shard_map/all_to_all | solution.py:231
  19.0 4.9 %collective-permute-start.2 = (bf16[2,128,256]{2,1,0:T(8,128)(2,1)S(1)}, bf16[2,128,256]{2,1,0:T(8,128)(2,1)S(1)}, u32[]{:S(2)}, u32[]{:S(2)}) collective-permute-start(bf16[2,128,256]{2,1,0:T(8,128)(2,1)S(1)} %bitcast.34), channel_id=1, source_target_pairs={{0,64},{1,65},{2,66},{3,67},{4,68},{5,69},{6,70},{7,71},{8,72},{9,... | collective-permute-start | bytes 393224 | tf_op jit(solution)/shard_map/ppermute | solution.py:215
  23.9 4.8 %collective-permute-start.1 = (bf16[8,128,256]{2,1,0:T(8,128)(2,1)S(1)}, bf16[8,128,256]{2,1,0:T(8,128)(2,1)S(1)}, u32[]{:S(2)}, u32[]{:S(2)}) collective-permute-start(bf16[8,128,256]{2,1,0:T(8,128)(2,1)S(1)} %bitcast.28), channel_id=1, source_target_pairs={{0,32},{1,33},{2,34},{3,35},{4,36},{5,37},{6,38},{7,39},{8,40},{9,... | collective-permute-start | bytes 1572872 | tf_op jit(solution)/shard_map/ppermute | solution.py:215
  28.7 6.3 %all-to-all-start.1 = ((bf16[32,64,256]{2,1,0:T(8,128)(2,1)}), bf16[32,64,256]{2,1,0:T(8,128)(2,1)S(1)}, u32[]{:S(2)}, u32[]{:S(2)}) async-start(bf16[32,64,256]{2,1,0:T(8,128)(2,1)} %bitcast.25), calls=%async_computation.1 | async-start | bytes 2097152 | tf_op jit(solution)/shard_map/all_to_all | solution.py:243
  35.0 0.1 convert_reduce_fusion.1
  35.1 0.0 collective-permute-done.2.tail_m
  35.1 2.3 %collective-permute-start.3 = (bf16[2,128,256]{2,1,0:T(8,128)(2,1)S(1)}, bf16[2,128,256]{2,1,0:T(8,128)(2,1)S(1)}, u32[]{:S(2)}, u32[]{:S(2)}) collective-permute-start(bf16[2,128,256]{2,1,0:T(8,128)(2,1)S(1)} %collective-permute-done.2.tail_m), channel_id=1, source_target_pairs={{0,1},{1,0},{2,3},{3,2},{4,5},{5,4},{6,7},{7,6},{8,9},{9,8},{10,11... | collective-permute-start | bytes 393224 | tf_op jit(solution)/shard_map/ppermute | solution.py:215
  37.4 0.7 slice.18
  38.8 2.1 %collective-permute-start = (bf16[8,128,256]{2,1,0:T(8,128)(2,1)S(1)}, bf16[8,128,256]{2,1,0:T(8,128)(2,1)S(1)}, u32[]{:S(2)}, u32[]{:S(2)}) collective-permute-start(bf16[8,128,256]{2,1,0:T(8,128)(2,1)S(1)} %bitcast.29), channel_id=1, source_target_pairs={{0,1},{1,0},{2,3},{3,2},{4,5},{5,4},{6,7},{7,6},{8,9},{9,8},{10,11... | collective-permute-start | bytes 1572872 | tf_op jit(solution)/shard_map/ppermute | solution.py:215
  40.8 0.0 collective-permute-done.3.tail_o
  40.8 0.0 collective-permute-done.1.prev_m
  40.8 2.3 %collective-permute-start.4 = (bf16[8,128,256]{2,1,0:T(8,128)(2,1)S(1)}, bf16[8,128,256]{2,1,0:T(8,128)(2,1)S(1)}, u32[]{:S(2)}, u32[]{:S(2)}) collective-permute-start(bf16[8,128,256]{2,1,0:T(8,128)(2,1)S(1)} %collective-permute-done.1.prev_m), channel_id=1, source_target_pairs={{0,1},{1,0},{2,3},{3,2},{4,5},{5,4},{6,7},{7,6},{8,9},{9,8},{10,11... | collective-permute-start | bytes 1572872 | tf_op jit(solution)/shard_map/ppermute | solution.py:215
  43.1 0.1 pad_add_fusion.1.info
  43.2 0.1 select_reduce_fusion.1
  43.3 0.7 compare_select_fusion.6
  44.0 0.0 collective-permute-done.own_o
  44.0 8.0 %all-to-all-done.1 = bf16[32,64,256]{2,1,0:T(8,128)(2,1)S(1)} async-done(((bf16[32,64,256]{2,1,0:T(8,128)(2,1)}), bf16[32,64,256]{2,1,0:T(8,128)(2,1)S(1)}, u32[]{:S(2)}, u32[]{:S(2)}) %all-to-all-start.1) | async-done | bytes 1048608 | tf_op jit(solution)/shard_map/all_to_all | solution.py:243
  52.0 0.0 collective-permute-done.4.prev_o
  52.0 15.0 %shard_map.47 = bf16[2048,256]{1,0:T(8,128)(2,1)S(1)} custom-call(s32[3,32]{1,0:T(4,128)S(1)} %pad_add_fusion.items, s32[2]{0:T(128)S(1)} %pad_add_fusion.1.info, bf16[2048,256]{1,0:T(8,128)(2,1)S(1)} %bitcast.26, s32[8,1,256]{2,1,0:T(1,128)S(1)} %bitcast.31, bf16[8,128,256]{2,1,0:T(8,128)(2,1)S(1)} %bitcast.30, ...), custom_call_target="tpu_custom_call" | custom-call | flops 10000000000 | bytes 8388608 | tf_op jit(solution)/shard_map/pallas_call | solution.py:135
  67.0 20.6 %all_to_all.15 = bf16[32,64,256]{2,1,0:T(8,128)(2,1)S(1)} all-to-all(bf16[32,64,256]{2,1,0:T(8,128)(2,1)S(1)} %bitcast.27), channel_id=1, replica_groups=mesh['z'=16,'x'=4,'y'=4,'core'=2] {'x','y','core'}, dimensions={0} | all-to-all | bytes 2097152 | tf_op jit(solution)/shard_map/all_to_all | solution.py:247
  87.7 1.0 %copy.10 = bf16[32,8,8,256]{3,2,0,1:T(8,128)(2,1)} copy(bf16[32,8,8,256]{3,2,1,0:T(8,128)(2,1)S(1)} %bitcast.32) | data formatting | bytes 2097152 | tf_op jit(solution)/shard_map/reshape | solution.py:248
  (7 shorter events, 0.1 us)
Async XLA Ops:
  0.0 8.7 %copy-start.1 = (s32[32768]{0:T(1024)S(1)}, s32[32768]{0:T(1024)}, u32[]{:S(2)}) copy-start(s32[32768]{0:T(1024)} %param.7) | copy-start | bytes 393220
  0.0 12.8 %copy-start = (bf16[64,8192]{1,0:T(8,128)(2,1)S(1)}, bf16[64,8192]{1,0:T(8,128)(2,1)}, u32[]{:S(2)}) copy-start(bf16[64,8192]{1,0:T(8,128)(2,1)} %param.4) | copy-start | bytes 3145732
  1.9 17.1 %all-to-all-start = ((bf16[16,64,256]{2,1,0:T(8,128)(2,1)}), bf16[16,64,256]{2,1,0:T(8,128)(2,1)S(1)}, u32[]{:S(2)}, u32[]{:S(2)}) async-start(bf16[16,64,256]{2,1,0:T(8,128)(2,1)} %shard_map.46), calls=%async_computation | async-start | bytes 1048576 | tf_op jit(solution)/shard_map/all_to_all | solution.py:231
  19.0 16.1 %collective-permute-start.2 = (bf16[2,128,256]{2,1,0:T(8,128)(2,1)S(1)}, bf16[2,128,256]{2,1,0:T(8,128)(2,1)S(1)}, u32[]{:S(2)}, u32[]{:S(2)}) collective-permute-start(bf16[2,128,256]{2,1,0:T(8,128)(2,1)S(1)} %bitcast.34), channel_id=1, source_target_pairs={{0,64},{1,65},{2,66},{3,67},{4,68},{5,69},{6,70},{7,71},{8,72},{9,... | collective-permute-start | bytes 393224 | tf_op jit(solution)/shard_map/ppermute | solution.py:215
  23.9 16.9 %collective-permute-start.1 = (bf16[8,128,256]{2,1,0:T(8,128)(2,1)S(1)}, bf16[8,128,256]{2,1,0:T(8,128)(2,1)S(1)}, u32[]{:S(2)}, u32[]{:S(2)}) collective-permute-start(bf16[8,128,256]{2,1,0:T(8,128)(2,1)S(1)} %bitcast.28), channel_id=1, source_target_pairs={{0,32},{1,33},{2,34},{3,35},{4,36},{5,37},{6,38},{7,39},{8,40},{9,... | collective-permute-start | bytes 1572872 | tf_op jit(solution)/shard_map/ppermute | solution.py:215
  28.7 23.3 %all-to-all-start.1 = ((bf16[32,64,256]{2,1,0:T(8,128)(2,1)}), bf16[32,64,256]{2,1,0:T(8,128)(2,1)S(1)}, u32[]{:S(2)}, u32[]{:S(2)}) async-start(bf16[32,64,256]{2,1,0:T(8,128)(2,1)} %bitcast.25), calls=%async_computation.1 | async-start | bytes 2097152 | tf_op jit(solution)/shard_map/all_to_all | solution.py:243
  35.1 5.7 %collective-permute-start.3 = (bf16[2,128,256]{2,1,0:T(8,128)(2,1)S(1)}, bf16[2,128,256]{2,1,0:T(8,128)(2,1)S(1)}, u32[]{:S(2)}, u32[]{:S(2)}) collective-permute-start(bf16[2,128,256]{2,1,0:T(8,128)(2,1)S(1)} %collective-permute-done.2.tail_m), channel_id=1, source_target_pairs={{0,1},{1,0},{2,3},{3,2},{4,5},{5,4},{6,7},{7,6},{8,9},{9,8},{10,11... | collective-permute-start | bytes 393224 | tf_op jit(solution)/shard_map/ppermute | solution.py:215
  38.8 5.2 %collective-permute-start = (bf16[8,128,256]{2,1,0:T(8,128)(2,1)S(1)}, bf16[8,128,256]{2,1,0:T(8,128)(2,1)S(1)}, u32[]{:S(2)}, u32[]{:S(2)}) collective-permute-start(bf16[8,128,256]{2,1,0:T(8,128)(2,1)S(1)} %bitcast.29), channel_id=1, source_target_pairs={{0,1},{1,0},{2,3},{3,2},{4,5},{5,4},{6,7},{7,6},{8,9},{9,8},{10,11... | collective-permute-start | bytes 1572872 | tf_op jit(solution)/shard_map/ppermute | solution.py:215
  40.8 11.1 %collective-permute-start.4 = (bf16[8,128,256]{2,1,0:T(8,128)(2,1)S(1)}, bf16[8,128,256]{2,1,0:T(8,128)(2,1)S(1)}, u32[]{:S(2)}, u32[]{:S(2)}) collective-permute-start(bf16[8,128,256]{2,1,0:T(8,128)(2,1)S(1)} %collective-permute-done.1.prev_m), channel_id=1, source_target_pairs={{0,1},{1,0},{2,3},{3,2},{4,5},{5,4},{6,7},{7,6},{8,9},{9,8},{10,11... | collective-permute-start | bytes 1572872 | tf_op jit(solution)/shard_map/ppermute | solution.py:215

commit v5 on v3

v5 whole, which is shorter than its diff:
```python
import functools
import math

import jax
import jax.numpy as jnp
from jax import lax
from jax.experimental import pallas as pl
from jax.experimental.pallas import tpu as pltpu
from jax.sharding import Mesh
from jax.sharding import PartitionSpec as P

HD = 128
GRAN = 256
BACK = 10
OWN = 8
PARTS = 2
TILES = OWN // PARTS
SPAN = 4
PAD = SPAN - 1
HALF = GRAN // 2
CHUNK = 64
HEADS = 2
COLS = HEADS * GRAN
ONES = 16
AXES = ("z", "x", "y", "core")
FACTOR = math.log2(math.e) / math.sqrt(HD)
HIDDEN = -2.0e30
FAR = 1 << 20
VMEM = pltpu.VMEM


def work(part, items, info, starts_ref, ks, vt, qt, spot, acc, peak, sa, sb):
    piece = CHUNK // PARTS
    column = lax.broadcasted_iota(jnp.int32, (1, GRAN), 1)
    line = (column // piece) * CHUNK + part * piece + column % piece

    def scored(number, buffer):
        tile, first = items[0, number], items[1, number]
        keys = ks[pl.ds(first, SPAN)].reshape(SPAN * GRAN, 2 * HD)
        raw = jnp.dot(keys, qt[tile], preferred_element_type=jnp.float32)
        low = starts_ref[tile] - (first - PAD) * GRAN + items[2, number]
        upper = line + (BACK + PARTS * tile - (first - PAD)) * GRAN
        place = jnp.concatenate([spot[...]] * (COLS // HD), axis=1)
        best = None
        for k in range(SPAN):
            rows = slice(k * GRAN, (k + 1) * GRAN)
            seen = place >= jnp.concatenate([low - k * GRAN] * HEADS, axis=1)
            if k >= SPAN - PARTS:
                own = upper - k * GRAN
                seen = seen & (place <= jnp.concatenate([own] * HEADS, axis=1))
            piece = jnp.where(seen, raw[rows], HIDDEN)
            buffer[rows] = piece
            most = jnp.max(piece.reshape(GRAN // 8, 8, COLS), axis=0)
            best = most if best is None else jnp.maximum(best, most)
        return jnp.max(best, axis=0, keepdims=True)

    def finish(number, buffer, best):
        tile, first = items[0, number], items[1, number]
        before = peak[tile]
        top = jnp.maximum(before, best)
        peak[tile] = top
        weights = jnp.exp2(buffer[...] - top).astype(jnp.bfloat16)
        values = vt[:, pl.ds(pl.multiple_of(first * GRAN, GRAN), SPAN * GRAN)]
        mixed = jnp.dot(values, weights, preferred_element_type=jnp.float32)
        acc[tile] = acc[tile] * jnp.exp2(before - top) + mixed

    def both(pair, best):
        following = scored(2 * pair + 1, sb)
        finish(2 * pair, sa, best)
        best = scored(2 * pair + 2, sa)
        finish(2 * pair + 1, sb, following)
        return best

    lax.fori_loop(0, info[0], both, scored(0, sa))


def fill(groups, ks, vt, stage, sems):
    copies = []
    for first, half, source in groups:
        count, rows = source.shape[0], pl.ds(half * HALF, HALF)
        for part, there in (
            (0, ks.at[pl.ds(PAD + first, count), rows, pl.ds(0, HD)]),
            (0, ks.at[pl.ds(PAD + first, count), rows, pl.ds(HD, HD)]),
            (1, stage.at[pl.ds(first, count), rows, :]),
        ):
            copy = pltpu.make_async_copy(source.at[:, :, pl.ds(part * HD, HD)], there, sems.at[len(copies)])
            copy.start()
            copies.append(copy)
    granules = stage.shape[0]
    ks[:PAD] = jnp.zeros((PAD, GRAN, 2 * HD), jnp.bfloat16)
    vt[:, :PAD * GRAN] = jnp.zeros((HD + ONES, PAD * GRAN), jnp.bfloat16)
    vt[HD:, PAD * GRAN:] = jnp.ones((ONES, granules * GRAN), jnp.bfloat16)
    return copies


def places(info, spot):
    row = lax.broadcasted_iota(jnp.int32, (GRAN, HD), 0)
    holder = jnp.where(info[1] == 0, row // HALF, 1 - row // HALF)
    inner = row % HALF
    spot[...] = (inner // CHUNK) * (2 * CHUNK) + holder * CHUNK + inner % CHUNK


def turn(granules, vt, stage):
    for g in range(granules):
        vt[:HD, (PAD + g) * GRAN:(PAD + g + 1) * GRAN] = stage[g].T


def attention(part, items, info, q_ref, starts_ref, o_ref, ks, vt, ready, qt, acc, peak, spot, sa, sb):
    places(info, spot)
    acc[...] = jnp.zeros_like(acc)
    peak[...] = jnp.full_like(peak, HIDDEN)
    piece = CHUNK // PARTS
    devices = GRAN // piece
    for tile in range(TILES):
        rows = q_ref[tile * devices:(tile + 1) * devices, part * piece:(part + 1) * piece, :].reshape(GRAN, HEADS * HD)
        for head in range(HEADS):
            cols = slice(head * GRAN, (head + 1) * GRAN)
            query = rows[:, head * HD:(head + 1) * HD].T.astype(jnp.float32) * FACTOR
            coarse = query.astype(jnp.bfloat16)
            qt[tile, :HD, cols] = coarse
            qt[tile, HD:, cols] = (query - coarse.astype(jnp.float32)).astype(jnp.bfloat16)
    ready()
    work(part, items, info, starts_ref, ks, vt, qt, spot, acc, peak, sa, sb)
    for tile in range(TILES):
        for head in range(HEADS):
            cols = slice(head * GRAN, (head + 1) * GRAN)
            o_ref[tile * GRAN:(tile + 1) * GRAN, head * HD:(head + 1) * HD] = (
                (acc[tile, :HD, cols] / acc[tile, HD:HD + 1, cols]).T.astype(jnp.bfloat16)
            )


def kernel(
    part, items, info, q_ref, starts_ref, own_m, own_o, prev_m, tail_m, older_o,
    o_ref, ks, vt, stage, sems, *rest,
):
    tail = BACK - OWN
    groups = (BACK, 0, own_m), (BACK, 1, own_o), (tail, 0, prev_m), (0, 0, tail_m), (0, 1, older_o)
    copies = fill(groups, ks, vt, stage, sems)

    def ready():
        for copy in copies:
            copy.wait()
        turn(BACK + OWN, vt, stage)

    attention(part, items, info, q_ref, starts_ref, o_ref, ks, vt, ready, *rest)


LIMIT = pltpu.CompilerParams(vmem_limit_bytes=24 * 1024 * 1024)
INSIDE = pl.BlockSpec(memory_space=VMEM)
ANYWHERE = pl.BlockSpec(memory_space=pl.ANY)
WINDOW = BACK + OWN
RESULT = jax.ShapeDtypeStruct((TILES * GRAN, HEADS * HD), jnp.bfloat16)
SCRATCH = [
    VMEM((PAD + WINDOW, GRAN, 2 * HD), jnp.bfloat16),
    VMEM((HD + ONES, (PAD + WINDOW) * GRAN), jnp.bfloat16),
    VMEM((WINDOW, GRAN, HD), jnp.bfloat16),
    pltpu.SemaphoreType.DMA((15,)),
    VMEM((TILES, 2 * HD, COLS), jnp.bfloat16),
    VMEM((TILES, HD + ONES, COLS), jnp.float32),
    VMEM((TILES, 1, COLS), jnp.float32),
    VMEM((GRAN, HD), jnp.int32),
    VMEM((SPAN * GRAN, COLS), jnp.float32),
    VMEM((SPAN * GRAN, COLS), jnp.float32),
]
COST = pl.CostEstimate(flops=3 * 10**10, bytes_accessed=4 << 20, transcendentals=0)


def attend(part, items, info, starts, queries, pieces):
    return pl.pallas_call(
        functools.partial(kernel, part),
        grid_spec=pltpu.PrefetchScalarGridSpec(
            num_scalar_prefetch=2,
            grid=(),
            in_specs=[INSIDE] * 2 + [ANYWHERE] * 5,
            out_specs=INSIDE,
            scratch_shapes=SCRATCH,
        ),
        out_shape=RESULT,
        compiler_params=LIMIT,
        cost_estimate=COST,
    )(items, info, queries, starts, *pieces)


def pack_kernel(k_ref, v_ref, o_ref):
    copies = o_ref.shape[0] * HD // k_ref.shape[1]
    for place in range(o_ref.shape[0]):
        cols = slice(place // copies * HD, (place // copies + 1) * HD)
        o_ref[place, :, :HD] = k_ref[:, cols]
        o_ref[place, :, HD:] = v_ref[:, cols]


def pack(keys, values, chips):
    return pl.pallas_call(
        pack_kernel,
        in_specs=[INSIDE] * 2,
        out_specs=INSIDE,
        out_shape=jax.ShapeDtypeStruct((chips, keys.shape[0], 2 * HD), jnp.bfloat16),
    )(keys, values)


def agenda(starts, core, room):
    tiles = jnp.arange(TILES, dtype=jnp.int32)
    tops = BACK + PARTS * tiles + PARTS - 1
    counts = (tops - starts[:, 0] // GRAN) // SPAN + 1
    ends = jnp.sum(jnp.where(tiles[None, :] <= tiles[:, None], counts[None, :], 0), axis=1)
    number = jnp.arange(room, dtype=jnp.int32)
    tile = jnp.minimum(jnp.sum(number[:, None] >= ends[None, :], axis=1, dtype=jnp.int32), TILES - 1)
    real = number < ends[-1]
    chosen = tile[:, None] == tiles[None, :]
    begin = jnp.sum(jnp.where(chosen, (ends - counts)[None, :], 0), axis=1)
    top = jnp.sum(jnp.where(chosen, tops[None, :], 0), axis=1)
    first = top - SPAN * jnp.where(real, number - begin, 0)
    items = jnp.stack([tile, first, jnp.where(real, 0, FAR)])
    return items, jnp.stack([(ends[-1] + 1) // 2, core])


def plans(doc_ids, first, core):
    plane = OWN * GRAN
    padded = jnp.concatenate([jnp.full((BACK * GRAN,), -1, jnp.int32), doc_ids])
    window = lax.dynamic_slice_in_dim(padded, first, (BACK + OWN) * GRAN, 0)
    ids = window[BACK * GRAN:]
    starts = jnp.sum(window[None, :] < ids[:, None], axis=1, dtype=jnp.int32)
    starts = starts.reshape(plane // CHUNK, PARTS, CHUNK // PARTS)
    parts = [starts[:, part].reshape(TILES, GRAN) for part in range(PARTS)]
    return [agenda(part, core, 16) + (part.reshape(TILES, 1, GRAN),) for part in parts]


def moved(value, sizes, there):
    zs, xs, ys, cores = sizes
    pairs = []
    for z in range(zs):
        for x in range(xs):
            for y in range(ys):
                for core in range(cores):
                    place = there(z, x, y, core)
                    if place is not None:
                        index = [((p[0] * xs + p[1]) * ys + p[2]) * cores + p[3] for p in ((z, x, y, core), place)]
                        pairs.append(tuple(index))
    return lax.ppermute(value, AXES, pairs)


def body(sizes, queries, keys, values, doc_ids):
    zs, xs, ys, cores = sizes
    chips = xs * ys
    teams = chips * cores
    tokens = queries.shape[0]
    plane = OWN * GRAN

    def swap(value):
        return moved(value, sizes, lambda z, x, y, core: (z, x, y, 1 - core))

    def later(value, planes):
        return moved(value, sizes, lambda z, x, y, core: (z + planes, x, y, core) if z + planes < zs else None)

    own_m = lax.all_to_all(pack(keys, values, chips), ("x", "y"), 0, 0, tiled=True).reshape(OWN, HALF, 2 * HD)
    prev_m = later(own_m, 1)
    tail_m = later(own_m[2 * OWN - BACK:], 2)
    own_o = swap(own_m)
    older_o = swap(jnp.concatenate([tail_m, prev_m]))

    wide = jnp.transpose(queries.reshape(tokens, teams, HEADS * HD), (1, 0, 2))
    wide, _ = lax.optimization_barrier((wide, own_m))
    local = lax.all_to_all(wide, ("x", "y", "core"), 0, 0, tiled=True)

    def returned(out):
        back = lax.all_to_all(out.reshape(teams, tokens // PARTS, HEADS * HD), ("x", "y", "core"), 0, 0, tiled=True)
        return jnp.transpose(back, (1, 0, 2)).reshape(tokens // PARTS, teams * HEADS * HD)

    agendas = plans(doc_ids, lax.axis_index("z") * plane, lax.axis_index("core"))
    pieces = (own_m, own_o, prev_m, tail_m, older_o)
    outs = [attend(part, *agendas[part], local, pieces) for part in range(PARTS)]
    front = returned(outs[0])
    rest, front = lax.optimization_barrier((outs[1], front))
    return jnp.concatenate([front, returned(rest)], axis=0)


def solution(mesh):
    sizes = (16, 4, 4, 2)
    grid = Mesh(mesh.devices.reshape(sizes), AXES)

    def run(*args):
        return body(sizes, *args)

    return jax.shard_map(
        run,
        mesh=grid,
        in_specs=(P(AXES, None), P(AXES, None), P(AXES, None), P()),
        out_specs=P(AXES, None),
        check_vma=False,
    )
```

time: 87.5 us -> 99.7 us (1.14)
  the two profiles are of different devices: /device:TPU:129 before, /device:TPU:161 now
where the time goes in v5:
time: 99.7 us; the launch traced here: 98.9 us
  starting transfers between devices  37.4 us (38%)
  Pallas kernels  20.7 us (21%)
  blocking collectives  17.2 us (17%)
  other arithmetic  7.84 us (8%)
  local copies, waits for them, and re-layouts  7.26 us (7%)
  waiting for transfers between devices  6.94 us (7%)
  between operations  1.56 us (2%)
    pallas_call x2, Pallas kernels, attend(): pl.pallas_call(functools.partial(kernel, part), grid_spec=pltpu.PrefetchS...  18.8 us
    all_to_all x1, blocking collectives, returned(): lax.all_to_all(out.reshape(teams, tokens // PARTS, HEADS * HD), ('x', 'y'...  17.2 us
    ppermute x4, starting transfers between devices, moved(): return lax.ppermute(value, AXES, pairs)  16.1 us
    all_to_all x1, starting transfers between devices, returned(): lax.all_to_all(out.reshape(teams, tokens // PARTS, HEADS * HD), ('x', 'y'...  7.24 us
    all_to_all x1, starting transfers between devices, body(): local = lax.all_to_all(wide, ('x', 'y', 'core'), 0, 0, tiled=True)  7.22 us
    all_to_all x1, starting transfers between devices, body(): lax.all_to_all(pack(keys, values, chips), ('x', 'y'), 0, 0, tiled=True)  6.89 us
    ppermute x4, waiting for transfers between devices, moved(): return lax.ppermute(value, AXES, pairs)  4.03 us
    reduce_sum x1, other arithmetic, plans(): starts = jnp.sum(window[None, :] < ids[:, None], axis=1, dtype=jnp.int32)  3.81 us
  transfers between devices with their start and end apart: 7, of which 4 were waited for; matrix products, arithmetic and copies ran while one was open for 10% of the time, Pallas kernels for 9%

profile of v5, /device:TPU:161, one launch (start us, length us, event | category | flops | bytes accessed | tf_op | source)
XLA Modules:
  0.0 98.9 jit_solution(996281312038951721)
XLA Ops:
  0.0 1.9 %shard_map.46 = bf16[16,64,256]{2,1,0:T(8,128)(2,1)} custom-call(bf16[64,1024]{1,0:T(8,128)(2,1)} %k_ref.1, bf16[64,1024]{1,0:T(8,128)(2,1)} %v_ref.1), custom_call_target="tpu_custom_call" | custom-call | tf_op jit(solution)/shard_map/pallas_call | solution.py:193
  1.9 6.9 %all-to-all-start = ((bf16[16,64,256]{2,1,0:T(8,128)(2,1)}), bf16[16,64,256]{2,1,0:T(8,128)(2,1)S(1)}, u32[]{:S(2)}, u32[]{:S(2)}) async-start(bf16[16,64,256]{2,1,0:T(8,128)(2,1)} %shard_map.46), calls=%async_computation | async-start | bytes 1048576 | tf_op jit(solution)/shard_map/all_to_all | solution.py:255
  8.9 3.8 %convert_reduce_fusion = s32[2048]{0:T(1024)S(1)} fusion(s32[4608]{0:T(1024)S(1)} %pad_dynamic-slice_fusion.1, s32[2048]{0:T(1024)S(1)} %pad_dynamic-slice_fusion), kind=kLoop, calls=%fused_computation | loop fusion | flops 28309504 | bytes 34816 | tf_op jit(solution)/shard_map/reduce_sum | solution.py:222
  12.8 0.1 slice_reduce_fusion.2
  13.0 0.1 slice_reduce_fusion.1
  13.2 0.1 select_reduce_fusion.5
  13.4 0.1 slice_reduce_fusion
  13.5 0.1 select_reduce_fusion.2
  13.8 0.7 slice.32
  15.2 0.6 slice.37
  16.5 1.1 %copy.20 = bf16[8,32,8,256]{3,2,0,1:T(8,128)(2,1)} copy(bf16[8,32,8,256]{3,2,1,0:T(8,128)(2,1)S(1)} %bitcast.48) | data formatting | bytes 2097152 | tf_op jit(solution)/shard_map/reshape | solution.py:261
  17.8 1.3 %all-to-all-done = bf16[16,64,256]{2,1,0:T(8,128)(2,1)S(1)} async-done(((bf16[16,64,256]{2,1,0:T(8,128)(2,1)}), bf16[16,64,256]{2,1,0:T(8,128)(2,1)S(1)}, u32[]{:S(2)}, u32[]{:S(2)}) %all-to-all-start) | async-done | bytes 524320 | tf_op jit(solution)/shard_map/all_to_all | solution.py:255
  19.1 3.5 %collective-permute-start.1 = (bf16[8,128,256]{2,1,0:T(8,128)(2,1)S(1)}, bf16[8,128,256]{2,1,0:T(8,128)(2,1)S(1)}, u32[]{:S(2)}, u32[]{:S(2)}) collective-permute-start(bf16[8,128,256]{2,1,0:T(8,128)(2,1)S(1)} %bitcast.40), channel_id=1, source_target_pairs={{0,32},{1,33},{2,34},{3,35},{4,36},{5,37},{6,38},{7,39},{8,40},{9,... | collective-permute-start | bytes 1572872 | tf_op jit(solution)/shard_map/ppermute | solution.py:239
  22.7 7.2 %all-to-all-start.1 = ((bf16[32,64,256]{2,1,0:T(8,128)(2,1)}), bf16[32,64,256]{2,1,0:T(8,128)(2,1)S(1)}, u32[]{:S(2)}, u32[]{:S(2)}) async-start(bf16[32,64,256]{2,1,0:T(8,128)(2,1)} %bitcast.39), calls=%async_computation.1 | async-start | bytes 2097152 | tf_op jit(solution)/shard_map/all_to_all | solution.py:263
  30.0 6.1 %collective-permute-start.2 = (bf16[2,128,256]{2,1,0:T(8,128)(2,1)S(1)}, bf16[2,128,256]{2,1,0:T(8,128)(2,1)S(1)}, u32[]{:S(2)}, u32[]{:S(2)}) collective-permute-start(bf16[2,128,256]{2,1,0:T(8,128)(2,1)S(1)} %bitcast.49), channel_id=1, source_target_pairs={{0,64},{1,65},{2,66},{3,67},{4,68},{5,69},{6,70},{7,71},{8,72},{9,... | collective-permute-start | bytes 393224 | tf_op jit(solution)/shard_map/ppermute | solution.py:239
  36.1 0.7 compare_select_fusion.14
  36.8 2.9 %collective-permute-done.2.tail_m = bf16[2,128,256]{2,1,0:T(8,128)(2,1)S(1)} collective-permute-done((bf16[2,128,256]{2,1,0:T(8,128)(2,1)S(1)}, bf16[2,128,256]{2,1,0:T(8,128)(2,1)S(1)}, u32[]{:S(2)}, u32[]{:S(2)}) %collective-permute-start.2) | collective-permute-done | bytes 131104 | tf_op jit(solution)/shard_map/ppermute | solution.py:239
  39.7 0.9 pad_maximum_fusion.1
  40.6 4.5 %collective-permute-start.3 = (bf16[10,128,256]{2,1,0:T(8,128)(2,1)}, bf16[10,128,256]{2,1,0:T(8,128)(2,1)S(1)}, u32[]{:S(2)}, u32[]{:S(2)}) collective-permute-start(bf16[10,128,256]{2,1,0:T(8,128)(2,1)} %pad_maximum_fusion.1), channel_id=1, source_target_pairs={{0,1},{1,0},{2,3},{3,2},{4,5},{5,4},{6,7},{7,6},{8,9},{9,8},{10,11... | collective-permute-start | bytes 1966088 | tf_op jit(solution)/shard_map/ppermute | solution.py:239
  45.2 1.9 %collective-permute-start = (bf16[8,128,256]{2,1,0:T(8,128)(2,1)S(1)}, bf16[8,128,256]{2,1,0:T(8,128)(2,1)S(1)}, u32[]{:S(2)}, u32[]{:S(2)}) collective-permute-start(bf16[8,128,256]{2,1,0:T(8,128)(2,1)S(1)} %bitcast.41), channel_id=1, source_target_pairs={{0,1},{1,0},{2,3},{3,2},{4,5},{5,4},{6,7},{7,6},{8,9},{9,8},{10,11... | collective-permute-start | bytes 1572872 | tf_op jit(solution)/shard_map/ppermute | solution.py:239
  47.2 0.6 compare_select_fusion.12
  47.8 1.1 %collective-permute-done.own_o = bf16[8,128,256]{2,1,0:T(8,128)(2,1)S(1)} collective-permute-done((bf16[8,128,256]{2,1,0:T(8,128)(2,1)S(1)}, bf16[8,128,256]{2,1,0:T(8,128)(2,1)S(1)}, u32[]{:S(2)}, u32[]{:S(2)}) %collective-permute-start) | collective-permute-done | bytes 524320 | tf_op jit(solution)/shard_map/ppermute | solution.py:239
  49.0 0.8 copy-done
  49.8 1.0 %copy-done.1 = bf16[8,128,256]{2,1,0:T(8,128)(2,1)S(1)} copy-done((bf16[8,128,256]{2,1,0:T(8,128)(2,1)S(1)}, bf16[8,128,256]{2,1,0:T(8,128)(2,1)}, u32[]{:S(2)}) %copy-start.1) | copy-done | bytes 524312
  50.8 9.8 %shard_map.48 = bf16[1024,256]{1,0:T(8,128)(2,1)} custom-call(s32[3,16]{1,0:T(4,128)S(1)} %pad_add_fusion.1.items, s32[2]{0:T(128)S(1)} %pad_add_fusion.3.info, bf16[32,64,256]{2,1,0:T(8,128)(2,1)S(1)} %all-to-all-done.1.q_ref, s32[4,1,256]{2,1,0:T(1,128)S(1)} %reshape_reshape_squeeze.7.starts_ref, bf16[8,128,256]{2,1,0:T(8,128)(2,1)S(1)} %bitcast.42, ...), custom_call_target="tpu_custom_call" | custom-call | flops 30000001024 | bytes 4194304 | tf_op jit(solution)/shard_map/pallas_call | solution.py:169
  60.6 7.2 %all-to-all-start.2 = ((bf16[32,32,256]{2,1,0:T(8,128)(2,1)}), bf16[32,32,256]{2,1,0:T(8,128)(2,1)}, u32[]{:S(2)}, u32[]{:S(2)}) async-start(bf16[32,32,256]{2,1,0:T(8,128)(2,1)} %bitcast.14), calls=%async_computation.2 | async-start | bytes 1048576 | tf_op jit(solution)/shard_map/all_to_all | solution.py:266
  67.9 1.0 %copy-done.2 = bf16[8,128,256]{2,1,0:T(8,128)(2,1)S(1)} copy-done((bf16[8,128,256]{2,1,0:T(8,128)(2,1)S(1)}, bf16[8,128,256]{2,1,0:T(8,128)(2,1)}, u32[]{:S(2)}) %copy-start.2) | copy-done | bytes 524312
  68.9 9.0 %shard_map.47 = bf16[1024,256]{1,0:T(8,128)(2,1)S(1)} custom-call(s32[3,16]{1,0:T(4,128)S(1)} %pad_add_fusion.items, s32[2]{0:T(128)S(1)} %pad_add_fusion.2.info, bf16[32,64,256]{2,1,0:T(8,128)(2,1)S(1)} %all-to-all-done.1.q_ref, s32[4,1,256]{2,1,0:T(1,128)S(1)} %reshape_reshape_squeeze.6.starts_ref, bf16[8,128,256]{2,1,0:T(8,128)(2,1)S(1)} %bitcast.43, ...), custom_call_target="tpu_custom_call" | custom-call | flops 30000001024 | bytes 4194304 | tf_op jit(solution)/shard_map/pallas_call | solution.py:169
  78.0 1.6 %all-to-all-done.2 = bf16[32,32,256]{2,1,0:T(8,128)(2,1)} async-done(((bf16[32,32,256]{2,1,0:T(8,128)(2,1)}), bf16[32,32,256]{2,1,0:T(8,128)(2,1)}, u32[]{:S(2)}, u32[]{:S(2)}) %all-to-all-start.2) | async-done | bytes 524320 | tf_op jit(solution)/shard_map/all_to_all | solution.py:266
  79.6 1.1 %copy.17 = bf16[32,4,8,256]{3,2,0,1:T(8,128)(2,1)S(1)} copy(bf16[32,4,8,256]{3,2,1,0:T(8,128)(2,1)} %bitcast.22) | data formatting | bytes 1048576 | tf_op jit(solution)/shard_map/reshape | solution.py:267
  80.6 17.2 %all_to_all.20 = bf16[32,32,256]{2,1,0:T(8,128)(2,1)S(1)} all-to-all(bf16[32,32,256]{2,1,0:T(8,128)(2,1)S(1)} %bitcast.44), channel_id=1, replica_groups=mesh['z'=16,'x'=4,'y'=4,'core'=2] {'x','y','core'}, dimensions={0} | all-to-all | bytes 1048576 | tf_op jit(solution)/shard_map/all_to_all | solution.py:266
  97.9 1.0 %pad_maximum_fusion = bf16[64,8192]{1,0:T(8,128)(2,1)} fusion(bf16[32,8192]{1,0:T(8,128)(2,1)S(1)} %bitcast.47, bf16[32,8192]{1,0:T(8,128)(2,1)S(1)} %bitcast.46), kind=kLoop, calls=%fused_computation.2 | loop fusion | flops 2097152 | bytes 2097152 | tf_op jit(solution)/shard_map/concatenate | solution.py:274
  (33 shorter events, 1.2 us)
Async XLA Ops:
  0.0 8.8 %copy-start.4 = (s32[32768]{0:T(1024)S(1)}, s32[32768]{0:T(1024)}, u32[]{:S(2)}) copy-start(s32[32768]{0:T(1024)} %param.7) | copy-start | bytes 393220
  1.9 14.6 %copy-start.3 = (bf16[64,8192]{1,0:T(8,128)(2,1)S(1)}, bf16[64,8192]{1,0:T(8,128)(2,1)}, u32[]{:S(2)}) copy-start(bf16[64,8192]{1,0:T(8,128)(2,1)} %param.4) | copy-start | bytes 3145732
  1.9 17.2 %all-to-all-start = ((bf16[16,64,256]{2,1,0:T(8,128)(2,1)}), bf16[16,64,256]{2,1,0:T(8,128)(2,1)S(1)}, u32[]{:S(2)}, u32[]{:S(2)}) async-start(bf16[16,64,256]{2,1,0:T(8,128)(2,1)} %shard_map.46), calls=%async_computation | async-start | bytes 1048576 | tf_op jit(solution)/shard_map/all_to_all | solution.py:255
  19.1 20.6 %collective-permute-start.1 = (bf16[8,128,256]{2,1,0:T(8,128)(2,1)S(1)}, bf16[8,128,256]{2,1,0:T(8,128)(2,1)S(1)}, u32[]{:S(2)}, u32[]{:S(2)}) collective-permute-start(bf16[8,128,256]{2,1,0:T(8,128)(2,1)S(1)} %bitcast.40), channel_id=1, source_target_pairs={{0,32},{1,33},{2,34},{3,35},{4,36},{5,37},{6,38},{7,39},{8,40},{9,... | collective-permute-start | bytes 1572872 | tf_op jit(solution)/shard_map/ppermute | solution.py:239
  22.7 27.1 %all-to-all-start.1 = ((bf16[32,64,256]{2,1,0:T(8,128)(2,1)}), bf16[32,64,256]{2,1,0:T(8,128)(2,1)S(1)}, u32[]{:S(2)}, u32[]{:S(2)}) async-start(bf16[32,64,256]{2,1,0:T(8,128)(2,1)} %bitcast.39), calls=%async_computation.1 | async-start | bytes 2097152 | tf_op jit(solution)/shard_map/all_to_all | solution.py:263
  30.0 9.7 %collective-permute-start.2 = (bf16[2,128,256]{2,1,0:T(8,128)(2,1)S(1)}, bf16[2,128,256]{2,1,0:T(8,128)(2,1)S(1)}, u32[]{:S(2)}, u32[]{:S(2)}) collective-permute-start(bf16[2,128,256]{2,1,0:T(8,128)(2,1)S(1)} %bitcast.49), channel_id=1, source_target_pairs={{0,64},{1,65},{2,66},{3,67},{4,68},{5,69},{6,70},{7,71},{8,72},{9,... | collective-permute-start | bytes 393224 | tf_op jit(solution)/shard_map/ppermute | solution.py:239
  40.6 9.2 %collective-permute-start.3 = (bf16[10,128,256]{2,1,0:T(8,128)(2,1)}, bf16[10,128,256]{2,1,0:T(8,128)(2,1)S(1)}, u32[]{:S(2)}, u32[]{:S(2)}) collective-permute-start(bf16[10,128,256]{2,1,0:T(8,128)(2,1)} %pad_maximum_fusion.1), channel_id=1, source_target_pairs={{0,1},{1,0},{2,3},{3,2},{4,5},{5,4},{6,7},{7,6},{8,9},{9,8},{10,11... | collective-permute-start | bytes 1966088 | tf_op jit(solution)/shard_map/ppermute | solution.py:239
  45.2 3.8 %collective-permute-start = (bf16[8,128,256]{2,1,0:T(8,128)(2,1)S(1)}, bf16[8,128,256]{2,1,0:T(8,128)(2,1)S(1)}, u32[]{:S(2)}, u32[]{:S(2)}) collective-permute-start(bf16[8,128,256]{2,1,0:T(8,128)(2,1)S(1)} %bitcast.41), channel_id=1, source_target_pairs={{0,1},{1,0},{2,3},{3,2},{4,5},{5,4},{6,7},{7,6},{8,9},{9,8},{10,11... | collective-permute-start | bytes 1572872 | tf_op jit(solution)/shard_map/ppermute | solution.py:239
  49.0 0.8 copy-start
  49.8 1.0 %copy-start.1 = (bf16[8,128,256]{2,1,0:T(8,128)(2,1)S(1)}, bf16[8,128,256]{2,1,0:T(8,128)(2,1)}, u32[]{:S(2)}) copy-start(bf16[8,128,256]{2,1,0:T(8,128)(2,1)} %copy-done) | copy-start | bytes 1572868
  60.6 18.9 %all-to-all-start.2 = ((bf16[32,32,256]{2,1,0:T(8,128)(2,1)}), bf16[32,32,256]{2,1,0:T(8,128)(2,1)}, u32[]{:S(2)}, u32[]{:S(2)}) async-start(bf16[32,32,256]{2,1,0:T(8,128)(2,1)} %bitcast.14), calls=%async_computation.2 | async-start | bytes 1048576 | tf_op jit(solution)/shard_map/all_to_all | solution.py:266
  67.9 1.0 %copy-start.2 = (bf16[8,128,256]{2,1,0:T(8,128)(2,1)S(1)}, bf16[8,128,256]{2,1,0:T(8,128)(2,1)}, u32[]{:S(2)}) copy-start(bf16[8,128,256]{2,1,0:T(8,128)(2,1)} %copy-done) | copy-start | bytes 1572868

commit v6 on v3

--- a/solution.py
+++ b/solution.py
@@ -12,7 +12,7 @@
 GRAN = 256
 BACK = 10
 OWN = 8
-SPAN = 4
+SPAN = 2
 PAD = SPAN - 1
 HALF = GRAN // 2
 CHUNK = 64
@@ -56,31 +56,39 @@
         mixed = jnp.dot(values, weights, preferred_element_type=jnp.float32)
         acc[tile] = acc[tile] * jnp.exp2(before - top) + mixed
 
-    def both(pair, best):
-        following = scored(2 * pair + 1, sb)
-        finish(2 * pair, sa, best)
-        best = scored(2 * pair + 2, sa)
-        finish(2 * pair + 1, sb, following)
+    def both(first, best):
+        following = scored(first + 1, sb)
+        finish(first, sa, best)
+        best = scored(first + 2, sa)
+        finish(first + 1, sb, following)
         return best
 
-    lax.fori_loop(0, info[0], both, scored(0, sa))
+    def several(pairs, done, best):
+        def group(number, best):
+            for pair in range(pairs):
+                best = both(2 * (done + pairs * number + pair), best)
+            return best
+
+        groups = lax.div(info[0] - done, pairs)
+        return done + pairs * groups, lax.fori_loop(0, groups, group, best)
+
+    done, best = 0, scored(0, sa)
+    for pairs in (4, 2, 1):
+        done, best = several(pairs, done, best)
 
 
 def fill(info, groups, ks, vt, stage, spot, sems):
     copies = []
-    for first, count, pair in groups:
-        for half, source in enumerate(pair):
-            rows = pl.ds(half * HALF, HALF)
-            for part, there in (
-                (0, ks.at[pl.ds(PAD + first, count), rows, pl.ds(0, HD)]),
-                (0, ks.at[pl.ds(PAD + first, count), rows, pl.ds(HD, HD)]),
-                (1, stage.at[pl.ds(first, count), rows, :]),
-            ):
-                copy = pltpu.make_async_copy(
-                    source.at[:, :, pl.ds(part * HD, HD)], there, sems.at[len(copies)]
-                )
-                copy.start()
-                copies.append(copy)
+    for first, half, source in groups:
+        count, rows = source.shape[0], pl.ds(half * HALF, HALF)
+        for part, there in (
+            (0, ks.at[pl.ds(PAD + first, count), rows, pl.ds(0, HD)]),
+            (0, ks.at[pl.ds(PAD + first, count), rows, pl.ds(HD, HD)]),
+            (1, stage.at[pl.ds(first, count), rows, :]),
+        ):
+            copy = pltpu.make_async_copy(source.at[:, :, pl.ds(part * HD, HD)], there, sems.at[len(copies)])
+            copy.start()
+            copies.append(copy)
     granules = stage.shape[0]
     ks[:PAD] = jnp.zeros((PAD, GRAN, 2 * HD), jnp.bfloat16)
     vt[:, :PAD * GRAN] = jnp.zeros((HD + ONES, PAD * GRAN), jnp.bfloat16)
@@ -98,11 +106,11 @@
 
 
 def kernel(
-    items, info, q_ref, starts_ref, own_m, own_o, prev_m, prev_o, tail_m, tail_o,
+    items, info, q_ref, starts_ref, own_m, own_o, prev_m, tail_m, older_o,
     o_ref, qt, acc, peak, ks, vt, stage, spot, sa, sb, sems,
 ):
     tail = BACK - OWN
-    groups = (BACK, OWN, (own_m, own_o)), (tail, OWN, (prev_m, prev_o)), (0, tail, (tail_m, tail_o))
+    groups = (BACK, 0, own_m), (BACK, 1, own_o), (tail, 0, prev_m), (0, 0, tail_m), (0, 1, older_o)
     copies = fill(info, groups, ks, vt, stage, spot, sems)
     acc[...] = jnp.zeros_like(acc)
     peak[...] = jnp.full_like(peak, HIDDEN)
@@ -137,7 +145,7 @@
         grid_spec=pltpu.PrefetchScalarGridSpec(
             num_scalar_prefetch=2,
             grid=(),
-            in_specs=[INSIDE] * 2 + [ANYWHERE] * 6,
+            in_specs=[INSIDE] * 2 + [ANYWHERE] * 5,
             out_specs=INSIDE,
             scratch_shapes=[
                 VMEM((OWN, 2 * HD, COLS), jnp.bfloat16),
@@ -149,7 +157,7 @@
                 VMEM((GRAN, HD), jnp.int32),
                 VMEM((SPAN * GRAN, COLS), jnp.float32),
                 VMEM((SPAN * GRAN, COLS), jnp.float32),
-                pltpu.SemaphoreType.DMA((18,)),
+                pltpu.SemaphoreType.DMA((15,)),
             ],
         ),
         out_shape=jax.ShapeDtypeStruct((OWN * GRAN, HEADS * HD), jnp.bfloat16),
@@ -197,7 +205,7 @@
     starts = jnp.sum(window[None, :] < ids[:, None], axis=1, dtype=jnp.int32)
     lows = starts[::GRAN] // GRAN
     tiles = jnp.arange(OWN, dtype=jnp.int32)
-    items, info = agenda((BACK + tiles - lows) // SPAN + 1, BACK + tiles, 32, core)
+    items, info = agenda((BACK + tiles - lows) // SPAN + 1, BACK + tiles, 52, core)
     return items, info, starts.reshape(OWN, 1, GRAN)
 
 
@@ -231,17 +239,16 @@
     own_m = lax.all_to_all(pack(keys, values, chips), ("x", "y"), 0, 0, tiled=True).reshape(OWN, HALF, 2 * HD)
     prev_m = later(own_m, 1)
     tail_m = later(own_m[2 * OWN - BACK:], 2)
-    prev_m, tail_m = lax.optimization_barrier((prev_m, tail_m))
     own_o = swap(own_m)
-    prev_o = swap(prev_m)
-    tail_o = swap(tail_m)
+    older_m, own_o = lax.optimization_barrier((jnp.concatenate([tail_m, prev_m]), own_o))
+    older_o = swap(older_m)
 
     wide = jnp.transpose(queries.reshape(tokens, teams, HEADS * HD), (1, 0, 2))
     wide, _ = lax.optimization_barrier((wide, own_m))
     local = lax.all_to_all(wide, ("x", "y", "core"), 0, 0, tiled=True).reshape(plane, HEADS * HD)
 
     items, info, starts = plans(doc_ids, lax.axis_index("z") * plane, lax.axis_index("core"))
-    out = attend(items, info, local, starts, (own_m, own_o, prev_m, prev_o, tail_m, tail_o))
+    out = attend(items, info, local, starts, (own_m, own_o, prev_m, tail_m, older_o))
     back = lax.all_to_all(out.reshape(teams, tokens, HEADS * HD), ("x", "y", "core"), 0, 0, tiled=True)
     return jnp.transpose(back, (1, 0, 2)).reshape(tokens, teams * HEADS * HD)
 

time: 87.5 us -> 85.2 us (0.974)
  the two profiles are of different devices: /device:TPU:129 before, /device:TPU:193 now
where the time goes in v6:
time: 85.2 us; the launch traced here: 84.7 us
  starting transfers between devices  26.7 us (31%)
  blocking collectives  23.7 us (28%)
  Pallas kernels  14.4 us (17%)
  waiting for transfers between devices  10.4 us (12%)
  other arithmetic  5.76 us (7%)
  local copies, waits for them, and re-layouts  3.01 us (4%)
    all_to_all x1, blocking collectives, body(): lax.all_to_all(out.reshape(teams, tokens, HEADS * HD), ('x', 'y', 'core')...  23.7 us
    ppermute x4, starting transfers between devices, moved(): return lax.ppermute(value, AXES, pairs)  16.2 us
    pallas_call x1, Pallas kernels, attend(): pl.pallas_call(kernel, grid_spec=pltpu.PrefetchScalarGridSpec(num_scalar_...  12.5 us
    all_to_all x1, starting transfers between devices, body(): lax.all_to_all(pack(keys, values, chips), ('x', 'y'), 0, 0, tiled=True)  6.75 us
    ppermute x4, waiting for transfers between devices, moved(): return lax.ppermute(value, AXES, pairs)  5.07 us
    reduce_sum x1, other arithmetic, plans(): starts = jnp.sum(window[None, :] < ids[:, None], axis=1, dtype=jnp.int32)  3.81 us
    all_to_all x1, starting transfers between devices, body(): lax.all_to_all(wide, ('x', 'y', 'core'), 0, 0, tiled=True)  3.73 us
    all_to_all x1, waiting for transfers between devices, body(): lax.all_to_all(pack(keys, values, chips), ('x', 'y'), 0, 0, tiled=True)  3.71 us
  transfers between devices with their start and end apart: 6, of which 3 were waited for; matrix products, arithmetic and copies ran while one was open for 9% of the time, Pallas kernels for 0%

profile of v6, /device:TPU:193, one launch (start us, length us, event | category | flops | bytes accessed | tf_op | source)
XLA Modules:
  0.0 84.7 jit_solution(17041918794968156132)
XLA Ops:
  0.0 0.0 copy-start.1
  0.0 0.0 copy-start
  0.0 1.9 %shard_map.46 = bf16[16,64,256]{2,1,0:T(8,128)(2,1)} custom-call(bf16[64,1024]{1,0:T(8,128)(2,1)} %k_ref.1, bf16[64,1024]{1,0:T(8,128)(2,1)} %v_ref.1), custom_call_target="tpu_custom_call" | custom-call | tf_op jit(solution)/shard_map/pallas_call | solution.py:178
  1.9 6.8 %all-to-all-start = ((bf16[16,64,256]{2,1,0:T(8,128)(2,1)}), bf16[16,64,256]{2,1,0:T(8,128)(2,1)S(1)}, u32[]{:S(2)}, u32[]{:S(2)}) async-start(bf16[16,64,256]{2,1,0:T(8,128)(2,1)} %shard_map.46), calls=%async_computation | async-start | bytes 1048576 | tf_op jit(solution)/shard_map/all_to_all | solution.py:239
  8.7 0.0 copy-done.1
  8.7 0.1 pad_dynamic-slice_fusion.1
  8.8 0.1 pad_dynamic-slice_fusion
  8.9 3.8 %convert_reduce_fusion = s32[2048]{0:T(1024)S(1)} fusion(s32[4608]{0:T(1024)S(1)} %pad_dynamic-slice_fusion.1, s32[2048]{0:T(1024)S(1)} %pad_dynamic-slice_fusion), kind=kLoop, calls=%fused_computation | loop fusion | flops 28309504 | bytes 34816 | tf_op jit(solution)/shard_map/reduce_sum | solution.py:205
  12.7 0.1 slice.17
  12.8 0.1 select_reduce_fusion.2
  12.9 0.6 slice.18
  14.2 0.0 copy-done
  14.2 1.1 %copy.12 = bf16[8,32,8,256]{3,2,0,1:T(8,128)(2,1)} copy(bf16[8,32,8,256]{3,2,1,0:T(8,128)(2,1)S(1)} %bitcast.34) | data formatting | bytes 2097152 | tf_op jit(solution)/shard_map/reshape | solution.py:246
  15.3 3.7 %all-to-all-done = bf16[16,64,256]{2,1,0:T(8,128)(2,1)S(1)} async-done(((bf16[16,64,256]{2,1,0:T(8,128)(2,1)}), bf16[16,64,256]{2,1,0:T(8,128)(2,1)S(1)}, u32[]{:S(2)}, u32[]{:S(2)}) %all-to-all-start) | async-done | bytes 524320 | tf_op jit(solution)/shard_map/all_to_all | solution.py:239
  19.0 3.5 %collective-permute-start.1 = (bf16[8,128,256]{2,1,0:T(8,128)(2,1)S(1)}, bf16[8,128,256]{2,1,0:T(8,128)(2,1)S(1)}, u32[]{:S(2)}, u32[]{:S(2)}) collective-permute-start(bf16[8,128,256]{2,1,0:T(8,128)(2,1)S(1)} %bitcast.28), channel_id=1, source_target_pairs={{0,32},{1,33},{2,34},{3,35},{4,36},{5,37},{6,38},{7,39},{8,40},{9,... | collective-permute-start | bytes 1572872 | tf_op jit(solution)/shard_map/ppermute | solution.py:223
  22.5 4.3 %collective-permute-start.2 = (bf16[8,128,256]{2,1,0:T(8,128)(2,1)S(1)}, bf16[8,128,256]{2,1,0:T(8,128)(2,1)S(1)}, u32[]{:S(2)}, u32[]{:S(2)}) collective-permute-start(bf16[8,128,256]{2,1,0:T(8,128)(2,1)S(1)} %bitcast.29), channel_id=1, source_target_pairs={{0,1},{1,0},{2,3},{3,2},{4,5},{5,4},{6,7},{7,6},{8,9},{9,8},{10,11... | collective-permute-start | bytes 1572872 | tf_op jit(solution)/shard_map/ppermute | solution.py:223
  26.9 3.7 %all-to-all-start.1 = ((bf16[32,64,256]{2,1,0:T(8,128)(2,1)}), bf16[32,64,256]{2,1,0:T(8,128)(2,1)S(1)}, u32[]{:S(2)}, u32[]{:S(2)}) async-start(bf16[32,64,256]{2,1,0:T(8,128)(2,1)} %bitcast.32), calls=%async_computation.1 | async-start | bytes 2097152 | tf_op jit(solution)/shard_map/all_to_all | solution.py:248
  30.7 5.2 %collective-permute-start = (bf16[2,128,256]{2,1,0:T(8,128)(2,1)S(1)}, bf16[2,128,256]{2,1,0:T(8,128)(2,1)S(1)}, u32[]{:S(2)}, u32[]{:S(2)}) collective-permute-start(bf16[2,128,256]{2,1,0:T(8,128)(2,1)S(1)} %bitcast.35), channel_id=1, source_target_pairs={{0,64},{1,65},{2,66},{3,67},{4,68},{5,69},{6,70},{7,71},{8,72},{9,... | collective-permute-start | bytes 393224 | tf_op jit(solution)/shard_map/ppermute | solution.py:223
  35.9 0.1 pad_add_fusion.1.info
  36.0 0.1 convert_reduce_fusion.1
  36.0 5.1 %collective-permute-done.tail_m = bf16[2,128,256]{2,1,0:T(8,128)(2,1)S(1)} collective-permute-done((bf16[2,128,256]{2,1,0:T(8,128)(2,1)S(1)}, bf16[2,128,256]{2,1,0:T(8,128)(2,1)S(1)}, u32[]{:S(2)}, u32[]{:S(2)}) %collective-permute-start) | collective-permute-done | bytes 131104 | tf_op jit(solution)/shard_map/ppermute | solution.py:223
  41.1 0.0 collective-permute-done.1.prev_m
  41.1 0.9 %pad_maximum_fusion = bf16[10,128,256]{2,1,0:T(8,128)(2,1)} fusion(bf16[8,128,256]{2,1,0:T(8,128)(2,1)S(1)} %collective-permute-done.1.prev_m, bf16[2,128,256]{2,1,0:T(8,128)(2,1)S(1)} %collective-permute-done.tail_m), kind=kLoop, calls=%fused_computation.2 | loop fusion | flops 327680 | bytes 1310720 | tf_op jit(solution)/shard_map/concatenate | solution.py:243
  42.0 0.0 collective-permute-done.2.own_o
  42.0 3.2 %collective-permute-start.3 = (bf16[10,128,256]{2,1,0:T(8,128)(2,1)}, bf16[10,128,256]{2,1,0:T(8,128)(2,1)S(1)}, u32[]{:S(2)}, u32[]{:S(2)}) collective-permute-start(bf16[10,128,256]{2,1,0:T(8,128)(2,1)} %pad_maximum_fusion), channel_id=1, source_target_pairs={{0,1},{1,0},{2,3},{3,2},{4,5},{5,4},{6,7},{7,6},{8,9},{9,8},{10,11... | collective-permute-start | bytes 1966088 | tf_op jit(solution)/shard_map/ppermute | solution.py:223
  45.2 0.1 select_reduce_fusion.1
  45.3 0.6 compare_select_fusion.6
  45.9 1.6 %all-to-all-done.1 = bf16[32,64,256]{2,1,0:T(8,128)(2,1)S(1)} async-done(((bf16[32,64,256]{2,1,0:T(8,128)(2,1)}), bf16[32,64,256]{2,1,0:T(8,128)(2,1)S(1)}, u32[]{:S(2)}, u32[]{:S(2)}) %all-to-all-start.1) | async-done | bytes 1048608 | tf_op jit(solution)/shard_map/all_to_all | solution.py:248
  47.5 0.0 collective-permute-done.3.older_o
  47.5 12.5 %shard_map.47 = bf16[2048,256]{1,0:T(8,128)(2,1)S(1)} custom-call(s32[3,52]{1,0:T(4,128)S(1)} %pad_add_fusion.items, s32[2]{0:T(128)S(1)} %pad_add_fusion.1.info, bf16[2048,256]{1,0:T(8,128)(2,1)S(1)} %bitcast.26, s32[8,1,256]{2,1,0:T(1,128)S(1)} %bitcast.31, bf16[8,128,256]{2,1,0:T(8,128)(2,1)S(1)} %bitcast.30, ...), custom_call_target="tpu_custom_call" | custom-call | flops 10000000000 | bytes 8388608 | tf_op jit(solution)/shard_map/pallas_call | solution.py:143
  60.0 23.7 %all_to_all.15 = bf16[32,64,256]{2,1,0:T(8,128)(2,1)S(1)} all-to-all(bf16[32,64,256]{2,1,0:T(8,128)(2,1)S(1)} %bitcast.27), channel_id=1, replica_groups=mesh['z'=16,'x'=4,'y'=4,'core'=2] {'x','y','core'}, dimensions={0} | all-to-all | bytes 2097152 | tf_op jit(solution)/shard_map/all_to_all | solution.py:252
  83.7 1.0 %copy.10 = bf16[32,8,8,256]{3,2,0,1:T(8,128)(2,1)} copy(bf16[32,8,8,256]{3,2,1,0:T(8,128)(2,1)S(1)} %bitcast.33) | data formatting | bytes 2097152 | tf_op jit(solution)/shard_map/reshape | solution.py:253
  (6 shorter events, 0.1 us)
Async XLA Ops:
  0.0 8.7 %copy-start.1 = (s32[32768]{0:T(1024)S(1)}, s32[32768]{0:T(1024)}, u32[]{:S(2)}) copy-start(s32[32768]{0:T(1024)} %param.7) | copy-start | bytes 393220
  0.0 14.2 %copy-start = (bf16[64,8192]{1,0:T(8,128)(2,1)S(1)}, bf16[64,8192]{1,0:T(8,128)(2,1)}, u32[]{:S(2)}) copy-start(bf16[64,8192]{1,0:T(8,128)(2,1)} %param.4) | copy-start | bytes 3145732
  1.9 17.1 %all-to-all-start = ((bf16[16,64,256]{2,1,0:T(8,128)(2,1)}), bf16[16,64,256]{2,1,0:T(8,128)(2,1)S(1)}, u32[]{:S(2)}, u32[]{:S(2)}) async-start(bf16[16,64,256]{2,1,0:T(8,128)(2,1)} %shard_map.46), calls=%async_computation | async-start | bytes 1048576 | tf_op jit(solution)/shard_map/all_to_all | solution.py:239
  19.0 22.1 %collective-permute-start.1 = (bf16[8,128,256]{2,1,0:T(8,128)(2,1)S(1)}, bf16[8,128,256]{2,1,0:T(8,128)(2,1)S(1)}, u32[]{:S(2)}, u32[]{:S(2)}) collective-permute-start(bf16[8,128,256]{2,1,0:T(8,128)(2,1)S(1)} %bitcast.28), channel_id=1, source_target_pairs={{0,32},{1,33},{2,34},{3,35},{4,36},{5,37},{6,38},{7,39},{8,40},{9,... | collective-permute-start | bytes 1572872 | tf_op jit(solution)/shard_map/ppermute | solution.py:223
  22.5 19.5 %collective-permute-start.2 = (bf16[8,128,256]{2,1,0:T(8,128)(2,1)S(1)}, bf16[8,128,256]{2,1,0:T(8,128)(2,1)S(1)}, u32[]{:S(2)}, u32[]{:S(2)}) collective-permute-start(bf16[8,128,256]{2,1,0:T(8,128)(2,1)S(1)} %bitcast.29), channel_id=1, source_target_pairs={{0,1},{1,0},{2,3},{3,2},{4,5},{5,4},{6,7},{7,6},{8,9},{9,8},{10,11... | collective-permute-start | bytes 1572872 | tf_op jit(solution)/shard_map/ppermute | solution.py:223
  26.9 20.6 %all-to-all-start.1 = ((bf16[32,64,256]{2,1,0:T(8,128)(2,1)}), bf16[32,64,256]{2,1,0:T(8,128)(2,1)S(1)}, u32[]{:S(2)}, u32[]{:S(2)}) async-start(bf16[32,64,256]{2,1,0:T(8,128)(2,1)} %bitcast.32), calls=%async_computation.1 | async-start | bytes 2097152 | tf_op jit(solution)/shard_map/all_to_all | solution.py:248
  30.7 10.4 %collective-permute-start = (bf16[2,128,256]{2,1,0:T(8,128)(2,1)S(1)}, bf16[2,128,256]{2,1,0:T(8,128)(2,1)S(1)}, u32[]{:S(2)}, u32[]{:S(2)}) collective-permute-start(bf16[2,128,256]{2,1,0:T(8,128)(2,1)S(1)} %bitcast.35), channel_id=1, source_target_pairs={{0,64},{1,65},{2,66},{3,67},{4,68},{5,69},{6,70},{7,71},{8,72},{9,... | collective-permute-start | bytes 393224 | tf_op jit(solution)/shard_map/ppermute | solution.py:223
  42.0 5.5 %collective-permute-start.3 = (bf16[10,128,256]{2,1,0:T(8,128)(2,1)}, bf16[10,128,256]{2,1,0:T(8,128)(2,1)S(1)}, u32[]{:S(2)}, u32[]{:S(2)}) collective-permute-start(bf16[10,128,256]{2,1,0:T(8,128)(2,1)} %pad_maximum_fusion), channel_id=1, source_target_pairs={{0,1},{1,0},{2,3},{3,2},{4,5},{5,4},{6,7},{7,6},{8,9},{9,8},{10,11... | collective-permute-start | bytes 1966088 | tf_op jit(solution)/shard_map/ppermute | solution.py:223
